TPU v7x, 512 devices: a whole 4x8x8 slice. The times are simulated.
512 devices in a mesh: band: 16 (over y, core), fft: 32 (over z, x).
Axes of the slice: x: 4, y: 8, z: 8, core: 2. Of those that a mesh axis runs over, the one named last changes fastest.
Arguments:
- orbitals: float32 [2, 16, 65536], P(None, 'band', 'fft'), may hold values from -6 to 6
- stick_columns: int32 [1024], P('fft'), may hold values from 0 to 32400, as said below
- stick_depths: int32 [1024, 64], P('fft'), may hold values from 0 to 96, as said below
- potential: float32 [96, 32400], P('fft'), may hold values from -1.5 to 1.5
- projectors: float32 [2, 16, 65536], P(None, None, 'fft'), may hold values from -0.1875 to 0.1875
- atom_projectors: int32 [2, 8], replicated, may hold values from 0 to 15, as said below
- couplings: float32 [2, 8, 8], replicated, may hold values from -0.9 to 0.9
- slab_orbitals: float32 [2, 64, 65536], P(None, 'band', 'fft'), may hold values from -0.0234375 to 0.0234375
Outputs:
- applied: float32 [2, 16, 65536], P(None, 'band', 'fft')
- projected_h: float32 [2, 16, 64], P(None, 'band')
- projected_correlation: float32 [2, 16, 64], P(None, 'band')
Inputs may be any that keep to these rules, and one draw needn't show every extreme that they name: `stick_columns`: each device's block of 32 slots holds its sticks first and then empty slots marked 32400; every device holds 16 sticks or more, and some device exactly 32. The columns of all sticks are distinct and lie in the disk fx^2 + fy^2 <= 45^2 of signed frequencies about (0, 0); where the slots in all suffice, every column of the disk is a stick. `stick_depths`: A stick with l G-vectors lists the z indices -(l // 2), ..., l - 1 - l // 2 modulo 96, then 96 in the other slots, with l from 32 to 64; the first stick of every device has l = 64; empty stick slots hold only 96. `atom_projectors`: every projector index appears once.
All inputs are finite; a program needn't handle non-finite values.
Results may differ from a plain program's by a relative error of at most 0.000078.
Values sent between devices are 32-bit elements; how exact they have to be, the bound alone decides.
A program may use at most 128 MiB of HBM per device.

v0:
```python
import math

import jax
import jax.numpy as jnp
from jax import lax
from jax.sharding import PartitionSpec as P

NX = 180
NY = 180
NZ = 96
GZ = 64
RADIUS = 45


HIGHEST = lax.Precision.HIGHEST


def complex_table(length, sign, scale, rows_index, cols_index):
    product = rows_index[:, None] * cols_index[None, :] % length
    angles = product.astype(jnp.float32) * (2.0 * math.pi / length)
    cos_part = jnp.cos(angles) * scale
    sin_part = jnp.sin(angles) * (sign * scale)
    upper = jnp.stack([cos_part, sin_part], axis=1)
    lower = jnp.stack([-sin_part, cos_part], axis=1)
    return jnp.stack([upper, lower])


def conj_correlation(vectors, reference_rows):
    real_out = jnp.einsum(
        "ng,mg->nm", vectors[0], reference_rows[0], precision=HIGHEST
    ) + jnp.einsum("ng,mg->nm", vectors[1], reference_rows[1], precision=HIGHEST)
    imag_out = jnp.einsum(
        "ng,mg->nm", vectors[1], reference_rows[0], precision=HIGHEST
    ) - jnp.einsum("ng,mg->nm", vectors[0], reference_rows[1], precision=HIGHEST)
    return jnp.stack([real_out, imag_out])


def signed_freq(index, length):
    return jnp.where(index < (length + 1) // 2, index, index - length)


def kinetic_factor(stick_columns, stick_depths):
    column_x = signed_freq(stick_columns // NY, NX)
    column_y = signed_freq(stick_columns % NY, NY)
    depth = signed_freq(stick_depths, NZ)
    squared = (column_x * column_x + column_y * column_y)[:, None] + depth * depth
    return 0.5 / (RADIUS * RADIUS) * squared.astype(jnp.float32)


def shards(
    orbitals,
    stick_columns,
    stick_depths,
    potential,
    projectors,
    atom_projectors,
    couplings,
    slab_orbitals,
):
    plane_size = NX * NY
    capacity = stick_columns.shape[0]
    blocks = orbitals.shape[1]
    rows_kept = 2 * RADIUS + 1
    compact_size = rows_kept * NY
    valid = (stick_depths < NZ) & (stick_columns[:, None] < plane_size)
    mask = valid.reshape(-1).astype(jnp.float32)
    masked = orbitals * mask
    all_columns = lax.all_gather(stick_columns, "fft", axis=0, tiled=True)
    column_row = all_columns // NY
    kept_row = jnp.where(column_row <= RADIUS, column_row, column_row - (NX - rows_kept))
    compact_columns = jnp.where(
        all_columns < plane_size, kept_row * NY + all_columns % NY, compact_size
    )
    kept_index = jnp.arange(rows_kept, dtype=jnp.int32)
    kept_rows = jnp.where(kept_index <= RADIUS, kept_index, kept_index + (NX - rows_kept))
    full_z = jnp.arange(NZ, dtype=jnp.int32)
    full_x = jnp.arange(NX, dtype=jnp.int32)
    full_y = jnp.arange(NY, dtype=jnp.int32)
    selector = (stick_depths[:, :, None] == full_z[None, None, :]).astype(jnp.float32)
    coefs = masked.reshape(2, blocks, capacity, GZ)
    sticks = jnp.einsum("cbsj,sjk->cbks", coefs, selector, precision=HIGHEST)
    inv_z = complex_table(NZ, 1.0, 1.0 / NZ, full_z, full_z)
    fwd_z = complex_table(NZ, -1.0, 1.0, full_z, full_z)
    inv_x = complex_table(NX, 1.0, 1.0 / NX, kept_rows, full_x)
    fwd_x = complex_table(NX, -1.0, 1.0, full_x, kept_rows)
    inv_y = complex_table(NY, 1.0, 1.0 / NY, full_y, full_y)
    fwd_y = complex_table(NY, -1.0, 1.0, full_y, full_y)
    stick_field = jnp.einsum("cbks,ckdz->dbzs", sticks, inv_z, precision=HIGHEST)
    plane_potential = potential.reshape(-1, NX, NY)
    mixed = lax.all_to_all(stick_field, "fft", split_axis=2, concat_axis=3, tiled=True)
    count = mixed.shape[1]
    depth = mixed.shape[2]
    spread = (
        jnp.zeros((2, count, depth, compact_size + 1), jnp.float32)
        .at[:, :, :, compact_columns]
        .add(mixed)
    )
    grid = spread[:, :, :, :compact_size].reshape(2, count, depth, rows_kept, NY)
    grid = jnp.einsum("cbzxy,cydv->dbzxv", grid, inv_y, precision=HIGHEST)
    grid = jnp.einsum("cbzxv,cxdu->dbzuv", grid, inv_x, precision=HIGHEST)
    grid = grid * plane_potential[None, None]
    grid = jnp.einsum("cbzuv,cvdy->dbzuy", grid, fwd_y, precision=HIGHEST)
    grid = jnp.einsum("cbzuy,cudx->dbzxy", grid, fwd_x, precision=HIGHEST)
    result = grid.reshape(2, count, depth, compact_size)
    result = jnp.concatenate([result, jnp.zeros((2, count, depth, 1), jnp.float32)], axis=3)
    picked = jnp.take(result, compact_columns, axis=3)
    returned = lax.all_to_all(picked, "fft", split_axis=3, concat_axis=2, tiled=True)
    back = jnp.einsum("cbzs,czdk->dbks", returned, fwd_z, precision=HIGHEST)
    local = jnp.einsum("cbks,sjk->cbsj", back, selector, precision=HIGHEST)
    local = local.reshape(2, blocks, capacity * GZ) * mask
    kinetic = kinetic_factor(stick_columns, stick_depths).reshape(-1) * mask
    proj = lax.psum(conj_correlation(masked, projectors), "fft")
    nproj = projectors.shape[1]
    owner = (
        atom_projectors[:, :, None] == jnp.arange(nproj, dtype=jnp.int32)[None, None, :]
    ).astype(jnp.float32)
    dfull = jnp.einsum("aip,ail,alq->pq", owner, couplings, owner, precision=HIGHEST)
    coupled = jnp.einsum("cbq,pq->cbp", proj, dfull, precision=HIGHEST)
    first = jnp.einsum("bp,pg->bg", coupled[0], projectors[0], precision=HIGHEST)
    second = jnp.einsum("bp,pg->bg", coupled[1], projectors[1], precision=HIGHEST)
    third = jnp.einsum("bp,pg->bg", coupled[0], projectors[1], precision=HIGHEST)
    fourth = jnp.einsum("bp,pg->bg", coupled[1], projectors[0], precision=HIGHEST)
    applied = kinetic * masked + local + jnp.stack([first - second, third + fourth]) * mask
    piece = lax.all_gather(slab_orbitals, "band", axis=1, tiled=True)
    h_part = conj_correlation(applied, piece)
    s_part = conj_correlation(masked, piece)
    projected_h, projected_correlation = lax.psum((h_part, s_part), "fft")
    return (applied, projected_h, projected_correlation)


def solution(mesh):
    in_specs = (
        P(None, "band", "fft"),
        P("fft"),
        P("fft", None),
        P("fft", None),
        P(None, None, "fft"),
        P(),
        P(),
        P(None, "band", "fft"),
    )
    out_specs = (P(None, "band", "fft"), P(None, "band", None), P(None, "band", None))
    return jax.shard_map(shards, mesh=mesh, in_specs=in_specs, out_specs=out_specs, check_vma=False)
```

profile of v0, /device:TPU:48, one launch (start us, length us, event | category | flops | bytes accessed | tf_op | source)
XLA Modules:
  0.0 430.1 jit_solution(5285861536153259374)
XLA Ops:
  7.6 0.7 broadcast_compare_fusion
  8.3 0.8 fusion.118
  9.2 0.7 copy_multiply_fusion
  10.0 1.4 convolution_bitcast_fusion.7
  11.8 0.7 reshape.764
  12.6 13.3 %all-to-all-start = ((f32[32,1,192]{2,1,0:T(1,128)}), f32[32,1,192]{2,1,0:T(1,128)}, u32[]{:S(2)}, u32[]{:S(2)}) async-start(f32[32,1,192]{2,1,0:T(1,128)} %reshape.764), calls=%async_computation | async-start | bytes 65536 | tf_op jit(solution)/shard_map/all_to_all | solution.py:90
  25.9 0.7 copy.92
  27.7 74.7 %psum.21 = f32[2,16]{1,0:T(2,128)S(1)} all-reduce(f32[2,16]{1,0:T(2,128)S(1)} %bitcast.334), channel_id=1, replica_groups=mesh['band'=16,'fft'=32] {'fft'}, use_global_device_ids=true, to_apply=%region_1.2 | all-reduce | flops 32 | bytes 256 | tf_op jit(solution)/shard_map/psum | solution.py:112
  103.0 0.8 fusion.69
  103.8 0.8 fusion.63
  104.8 0.8 fusion.67
  105.6 0.8 fusion.58
  106.4 0.8 fusion.94
  107.2 0.8 fusion.57
  108.0 0.7 fusion.93
  109.2 1.1 sine_multiply_fusion.1
  110.3 0.9 fusion.100
  111.1 1.3 dynamic-slice
  113.3 14.2 %all-reduce.1 = s32[1024]{0:T(1024)S(1)} all-reduce(s32[1024]{0:T(1024)S(1)} %dynamic-update-slice), channel_id=1, replica_groups=mesh['band'=16,'fft'=32] {'fft'}, use_global_device_ids=true, to_apply=%add.1 | all-reduce | flops 1024 | bytes 8192
  127.6 0.7 fusion.116
  128.5 0.8 copy-done.3
  129.6 1.8 mul.675
  131.9 1.5 reduce
  133.6 1.3 copy.76
  134.9 6.0 %broadcast.797 = f32[2,3,16381]{1,0,2:T(2,128)} broadcast(f32[]{:T(128)} %constant.116.clone.1), dimensions={} | broadcast | bytes 393148 | tf_op jit(solution)/shard_map/broadcast_in_dim | solution.py:94
  140.9 100.4 %scatter_fusion = f32[2,3,16381]{1,0,2:T(2,128)} fusion(f32[2,3,16381]{1,0,2:T(2,128)} %broadcast.797, s32[1024]{0:T(1024)S(1)} %get-tuple-element.15, f32[1024,2,3]{2,1,0:T(2,128)} %copy.76), kind=kCustom, calls=%fused_computation.1 | custom fusion | flops 6144 | bytes 77824 | tf_op jit(solution)/shard_map/scatter-add | solution.py:96
  241.3 12.1 %slice.70 = f32[2,1,3,16380]{2,0,3,1:T(2,128)} slice(f32[2,1,3,16381]{2,0,3,1:T(2,128)} %bitcast.319), slice={[0:2], [0:1], [0:3], [0:16380]} | slice | bytes 786240 | tf_op jit(solution)/shard_map/slice | solution.py:98
  253.4 18.9 %copy.96 = f32[2,3,91,180,1]{3,2,0,1,4:T(8,128)S(1)} copy(f32[2,3,91,180,1]{1,0,3,2,4:T(2,128)} %bitcast.320) | data formatting | bytes 786240 | tf_op jit(solution)/shard_map/reshape.14
  272.3 1.4 convolution_bitcast_fusion.3
  273.7 1.1 fusion.1
  274.8 2.0 convolution_bitcast_fusion
  276.8 1.2 convolution_bitcast_fusion.2
  278.1 15.7 %copy.112 = f32[2,1,3,91,180]{2,0,4,3,1:T(2,128)} copy(f32[2,1,3,91,180]{3,4,2,0,1:T(8,128)S(1)} %convolution_bitcast_fusion.2) | data formatting | bytes 786240 | tf_op jit(solution)/shard_map/reshape | solution.py:104
  293.7 11.9 %pad_bitcast_fusion = f32[2,3,16381]{1,0,2:T(2,128)} fusion(f32[2,1,3,16380]{2,0,3,1:T(2,128)} %bitcast.321), kind=kLoop, calls=%fused_computation.2 | loop fusion | bytes 786264 | tf_op jit(solution)/shard_map/concatenate | solution.py:105
  305.6 9.3 %gather_fusion = f32[1024,2,3]{2,1,0:T(2,128)S(1)} fusion(f32[2,3,16381]{1,0,2:T(2,128)} %pad_bitcast_fusion, s32[1024]{0:T(1024)S(1)} %broadcast_clamp_fusion), kind=kCustom, calls=%fused_computation | custom fusion | bytes 53248 | tf_op jit(solution)/shard_map/jit(_take)/gather | solution.py:106
  314.9 3.7 fusion.142
  318.7 2.2 reshape.766
  321.0 8.8 %all-to-all-start.1 = ((f32[32,1,192]{2,1,0:T(1,128)}), f32[32,1,192]{2,1,0:T(1,128)S(1)}, u32[]{:S(2)}, u32[]{:S(2)}) async-start(f32[32,1,192]{2,1,0:T(1,128)} %reshape.766), calls=%async_computation.1 | async-start | bytes 65536 | tf_op jit(solution)/shard_map/all_to_all | solution.py:107
  329.9 9.5 %all-to-all-done.1 = f32[32,1,192]{2,1,0:T(1,128)S(1)} async-done(((f32[32,1,192]{2,1,0:T(1,128)}), f32[32,1,192]{2,1,0:T(1,128)S(1)}, u32[]{:S(2)}, u32[]{:S(2)}) %all-to-all-start.1) | async-done | bytes 24608 | tf_op jit(solution)/shard_map/all_to_all | solution.py:107
  339.4 0.7 reduce.1
  340.2 1.5 reshape.767
  341.7 0.6 copy.113
  342.8 1.0 convolution_bitcast_fusion.4
  343.9 0.6 copy.93
  344.5 2.6 fusion.141
  347.7 0.6 convolution_bitcast_fusion.15
  350.1 0.6 fusion.11
  351.9 71.4 %all-reduce.2 = (f32[2,1,64]{2,1,0:T(1,128)}, f32[2,1,64]{2,1,0:T(1,128)}) all-reduce(f32[2,1,64]{2,1,0:T(1,128)S(1)} %pad_maximum_fusion.1, f32[2,1,64]{2,1,0:T(1,128)S(1)} %pad_maximum_fusion.2), channel_id=1, replica_groups=mesh['band'=16,'fft'=32] {'fft'}, use_global_device_ids=true, to_apply=%region_2.3 | all-reduce | flops 256 | bytes 2048 | tf_op jit(solution)/shard_map/psum | solution.py:127
  (86 shorter events, 8.9 us)
Async XLA Ops:
  7.2 95.3 %copy-start = (f32[2,8,8]{2,1,0:T(8,128)S(1)}, f32[2,8,8]{2,1,0:T(8,128)}, u32[]{:S(2)}) copy-start(f32[2,8,8]{2,1,0:T(8,128)} %param.14) | copy-start | bytes 1540
  7.2 18.8 %copy-start.8 = (f32[2,4,2048]{2,1,0:T(4,128)S(1)}, f32[2,4,2048]{2,1,0:T(4,128)}, u32[]{:S(2)}) copy-start(f32[2,4,2048]{2,1,0:T(4,128)} %param.15) | copy-start | bytes 196612
  7.2 19.5 %copy-start.2 = (f32[2,16,2048]{2,1,0:T(8,128)S(1)}, f32[2,16,2048]{2,1,0:T(8,128)}, u32[]{:S(2)}) copy-start(f32[2,16,2048]{2,1,0:T(8,128)} %param.12) | copy-start | bytes 786436
  10.0 92.5 %copy-start.15 = (s32[2,8]{1,0:T(2,128)S(1)}, s32[2,8]{1,0:T(2,128)}, u32[]{:S(2)}) copy-start(s32[2,8]{1,0:T(2,128)} %param.13) | copy-start | bytes 196
  12.6 118.8 %all-to-all-start = ((f32[32,1,192]{2,1,0:T(1,128)}), f32[32,1,192]{2,1,0:T(1,128)}, u32[]{:S(2)}, u32[]{:S(2)}) async-start(f32[32,1,192]{2,1,0:T(1,128)} %reshape.764), calls=%async_computation | async-start | bytes 65536 | tf_op jit(solution)/shard_map/all_to_all | solution.py:90
  25.9 318.7 %all-gather.2.cloned.1.call-start = ((), (), s32[]{:S(2)}) async-start(), calls=%async_computation.2 | async-start | bytes 1114112 | tf_op jit(solution)/shard_map/all_gather | solution.py:124
  103.8 7.3 %copy-start.16 = (s32[32]{0:T(128)S(1)}, s32[32]{0:T(128)}, u32[]{:S(2)}) copy-start(s32[32]{0:T(128)} %param.9) | copy-start | bytes 388
  103.8 23.8 %copy-start.9 = (s32[32,64]{1,0:T(8,128)S(1)}, s32[32,64]{1,0:T(8,128)}, u32[]{:S(2)}) copy-start(s32[32,64]{1,0:T(8,128)} %param.10) | copy-start | bytes 24580
  128.4 0.9 copy-start.3
  128.4 0.9 copy-start.4
  314.9 14.9 %copy-start.5 = (f32[96,1,96]{2,0,1:T(8,128)S(1)}, f32[96,1,96]{2,0,1:T(8,128)}, u32[]{:S(2)}) copy-start(f32[96,1,96]{2,0,1:T(8,128)} %get-tuple-element.36) | copy-start | bytes 110596
  314.9 14.9 %copy-start.6 = (f32[96,1,96]{2,0,1:T(8,128)S(1)}, f32[96,1,96]{2,0,1:T(8,128)}, u32[]{:S(2)}) copy-start(f32[96,1,96]{2,0,1:T(8,128)} %get-tuple-element.37) | copy-start | bytes 110596
  318.7 11.2 %copy-start.11 = (f32[32,64]{1,0:T(8,128)S(1)}, f32[32,64]{1,0:T(8,128)}, u32[]{:S(2)}) copy-start(f32[32,64]{1,0:T(8,128)} %fusion.116) | copy-start | bytes 24580
  318.7 11.2 %copy-start.13 = (f32[1,2048]{1,0:T(1,128)S(1)}, f32[1,2048]{1,0:T(1,128)}, u32[]{:S(2)}) copy-start(f32[1,2048]{1,0:T(1,128)} %fusion.69) | copy-start | bytes 24580
  318.7 11.2 %copy-start.14 = (f32[1,2048]{1,0:T(1,128)S(1)}, f32[1,2048]{1,0:T(1,128)}, u32[]{:S(2)}) copy-start(f32[1,2048]{1,0:T(1,128)} %fusion.63) | copy-start | bytes 24580
  318.7 11.2 %copy-start.12 = (f32[1,2048]{1,0:T(1,128)S(1)}, f32[1,2048]{1,0:T(1,128)}, u32[]{:S(2)}) copy-start(f32[1,2048]{1,0:T(1,128)} %fusion.67) | copy-start | bytes 24580
  321.0 18.5 %all-to-all-start.1 = ((f32[32,1,192]{2,1,0:T(1,128)}), f32[32,1,192]{2,1,0:T(1,128)S(1)}, u32[]{:S(2)}, u32[]{:S(2)}) async-start(f32[32,1,192]{2,1,0:T(1,128)} %reshape.766), calls=%async_computation.1 | async-start | bytes 65536 | tf_op jit(solution)/shard_map/all_to_all | solution.py:107
  340.1 2.6 copy-start.10
  341.7 2.2 copy-start.7
  348.9 74.4 %copy-start.1 = (f32[2,8,8]{2,1,0:T(8,128)S(1)}, f32[2,8,8]{2,1,0:T(8,128)}, u32[]{:S(2)}) copy-start(f32[2,8,8]{2,1,0:T(8,128)} %param.14) | copy-start | bytes 1540
Sparse Core Ops, SparseCore 0:
  28.8 39.2 all-gather.1
where the time goes:
time: 437 us; the launch traced here: 430 us
  blocking collectives  160 us (37%)
  other arithmetic  116 us (27%)
  local copies, waits for them, and re-layouts  89.6 us (21%)
  starting transfers between devices  22.2 us (5%)
  matrix products  17.5 us (4%)
  between operations  15.3 us (4%)
  waiting for transfers between devices  9.48 us (2%)
    scatter-add x1, other arithmetic, shards(): spread = jnp.zeros((2, count, depth, compact_size + 1), jnp.float32).at[:...  100 us
    psum x1, blocking collectives, shards(): proj = lax.psum(conj_correlation(masked, projectors), 'fft')  74.7 us
    psum x1, blocking collectives, shards(): projected_h, projected_correlation = lax.psum((h_part, s_part), 'fft')  71.4 us
    another operation x2, local copies, waits for them, and re-layouts  19 us
    reshape x1, local copies, waits for them, and re-layouts, shards(): result = grid.reshape(2, count, depth, compact_size)  15.7 us
    unnamed x1, blocking collectives  14.2 us
    all_to_all x1, starting transfers between devices, shards(): lax.all_to_all(stick_field, 'fft', split_axis=2, concat_axis=3, tiled=True)  13.3 us
    slice x1, local copies, waits for them, and re-layouts, shards(): spread[:, :, :, :compact_size].reshape(2, count, depth, rows_kept, NY)  12.1 us
  transfers between devices with their start and end apart: 3, of which 1 were waited for; matrix products, arithmetic and copies ran while one was open for 49% of the time, Pallas kernels for 0%

commit v1 on v0

v1 whole, which is shorter than its diff:
```python
import functools
import math

import jax
import jax.numpy as jnp
import numpy as np
from jax import lax
from jax.experimental import pallas as pl
from jax.experimental.pallas import tpu as pltpu
from jax.sharding import PartitionSpec as P

NX = 180
NY = 180
NZ = 96
GZ = 64
RADIUS = 45
NXY = NX * NY
NF = 32
STK = 32
KX = 96
KY = 128
U = 192
V = 256
PLANES = 3

MESH = pl.DeviceIdType.MESH
HIGH = lax.Precision.HIGH
HIGHEST = lax.Precision.HIGHEST
F32 = jnp.float32
BF16 = jnp.bfloat16
NN = (((1,), (0,)), ((), ()))
NT = (((1,), (1,)), ((), ()))


def mm(a, b, dims=NN, precision=HIGH):
    return lax.dot_general(a, b, dims, precision=precision, preferred_element_type=F32)


@functools.lru_cache(maxsize=None)
def tables():
    tau = 2.0 * math.pi
    j = np.arange(GZ)
    t1 = np.zeros((NF, 8, 2, GZ))
    t2 = np.zeros((NF, 8, 2, GZ))
    tb = np.zeros((2, GZ, 2, NF, 8))
    turn = np.zeros((2, NF, 8, 128))
    depth = np.arange(NZ + 1)
    for d in range(NF):
        for zz in range(PLANES):
            z = PLANES * d + zz
            th = tau * (j * z % NZ) / NZ
            c, s = np.cos(th), np.sin(th)
            t1[d, 2 * zz, 0], t1[d, 2 * zz, 1] = c, -s
            t1[d, 2 * zz + 1, 0], t1[d, 2 * zz + 1, 1] = s, c
            t2[d, 2 * zz, 0], t2[d, 2 * zz, 1] = -s, -c
            t2[d, 2 * zz + 1, 0], t2[d, 2 * zz + 1, 1] = c, -s
            tb[0, :, 0, d, 2 * zz], tb[0, :, 0, d, 2 * zz + 1] = c, s
            tb[0, :, 1, d, 2 * zz], tb[0, :, 1, d, 2 * zz + 1] = -s, c
            tb[1, :, 0, d, 2 * zz], tb[1, :, 0, d, 2 * zz + 1] = -s, c
            tb[1, :, 1, d, 2 * zz], tb[1, :, 1, d, 2 * zz + 1] = -c, -s
            ph = tau * (depth * z % NZ) / NZ
            turn[0, d, 2 * zz : 2 * zz + 2, : NZ + 1] = np.cos(ph)
            turn[1, d, 2 * zz : 2 * zz + 2, : NZ + 1] = np.sin(ph)
    t1, t2 = t1 / NZ, t2 / NZ
    k = np.arange(2 * RADIUS + 1) - RADIUS
    g = np.arange(NX)
    ang = tau * ((k[:, None] * g[None, :]) % NX) / NX
    c, s = np.cos(ang), np.sin(ang)
    n = 2 * RADIUS + 1
    wiy = np.zeros((2, KY, 2, V))
    wiy[0, :n, 0, :NY], wiy[0, :n, 1, :NY] = c / NY, s / NY
    wiy[1, :n, 0, :NY], wiy[1, :n, 1, :NY] = -s / NY, c / NY
    wix = np.zeros((2, U, 2, KX))
    wix[0, :NX, 0, :n], wix[0, :NX, 1, :n] = c.T / NX, -s.T / NX
    wix[1, :NX, 0, :n], wix[1, :NX, 1, :n] = s.T / NX, c.T / NX
    wfy = np.zeros((2, V, 2, KY))
    wfy[0, :NY, 0, :n], wfy[0, :NY, 1, :n] = c.T, -s.T
    wfy[1, :NY, 0, :n], wfy[1, :NY, 1, :n] = s.T, c.T
    wfx = np.zeros((2, KX, 2, U))
    wfx[0, :n, 0, :NX], wfx[0, :n, 1, :NX] = c, s
    wfx[1, :n, 0, :NX], wfx[1, :n, 1, :NX] = -s, c
    out = (
        t1.reshape(256, 128),
        t2.reshape(256, 128),
        turn.reshape(2, 256, 128),
        wiy.reshape(2 * KY, 2 * V),
        wix.reshape(2 * U, 2 * KX),
        wfy.reshape(2 * V, 2 * KY),
        wfx.reshape(2 * KX, 2 * U),
        tb.transpose(0, 1, 2, 3, 4).reshape(2, GZ, 2, 256),
    )
    back = out[7]
    back = np.transpose(back, (2, 1, 0, 3)).reshape(2 * GZ, 512)
    return tuple(np.asarray(x, np.float32) for x in out[:7]) + (np.asarray(back, np.float32),)


def kernel(
    orb, cols, deps, pot, proj, atoms, coup, slab,
    t1, t2, turn, wiy, wix, wfy, wfx, tback,
    out, out_h, out_s,
    mine, got, tiles, ret, pool, red, work, nonl, rows_s,
    sa, ra, sb, rb, ss, rs, sf, rf, sr, rr,
):
    me = lax.axis_index("fft")
    band = lax.axis_index("band")
    core = lax.rem(band, 2)
    row = band // 2
    twin = band + 1 - 2 * core

    barrier = pltpu.get_barrier_semaphore()

    def greet_fft(k, _):
        pl.semaphore_signal(barrier, inc=1, device_id={"fft": lax.rem(me + k, NF)}, device_id_type=MESH)
        return 0

    def greet_band(k, _):
        pl.semaphore_signal(barrier, inc=1, device_id={"band": lax.rem(band + 2 * k, 16)}, device_id_type=MESH)
        return 0

    lax.fori_loop(1, NF, greet_fft, 0)
    lax.fori_loop(1, 8, greet_band, 0)
    pl.semaphore_signal(barrier, inc=1, device_id={"band": twin}, device_id_type=MESH)

    pool[core, row] = jnp.concatenate([slab[0], slab[1]], axis=0)

    dep_even = deps[pl.ds(0, 16, stride=2), :]
    dep_odd = deps[pl.ds(1, 16, stride=2), :]
    dep16 = jnp.concatenate([dep_even, dep_odd], axis=1)
    mask = dep16 < NZ
    m_re = jnp.where(mask, orb[0], 0.0)
    m_im = jnp.where(mask, orb[1], 0.0)
    x2 = jnp.concatenate(
        [
            jnp.concatenate([m_re[:, :GZ], m_im[:, :GZ]], axis=1),
            jnp.concatenate([m_re[:, GZ:], m_im[:, GZ:]], axis=1),
        ],
        axis=0,
    )
    x2 = jnp.concatenate([x2, jnp.zeros((96, 128), F32)], axis=0)
    d1 = mm(t1[...], x2, NT)
    d2 = mm(t2[...], x2, NT)

    dep32 = jnp.concatenate([dep_even, dep_odd], axis=0).astype(F32)
    first = (lax.broadcasted_iota(jnp.int32, (8, GZ), 1) == 0).astype(F32)
    dep0 = mm(first, dep32, NT)
    dep0 = jnp.concatenate([dep0, jnp.full((8, 96), -1.0, F32)], axis=1)
    hot = (lax.broadcasted_iota(jnp.int32, (128, 128), 0).astype(F32) == dep0[0:1, :]).astype(F32)
    cosp = mm(turn[0], hot)
    sinp = mm(turn[1], hot)

    colf = cols[...].astype(F32)
    qx = jnp.floor((colf + 0.5) * (1.0 / NY))
    qy = colf - NY * qx
    live = cols[...] < NXY
    kx = jnp.where(live, jnp.where(qx < 90.0, qx, qx - NX) + RADIUS, -1.0)
    ky = jnp.where(live, jnp.where(qy < 90.0, qy, qy - NY) + RADIUS, -1.0)
    si = lax.broadcasted_iota(jnp.int32, (STK, STK), 0)
    so = lax.broadcasted_iota(jnp.int32, (STK, STK), 1)
    perm = (si == 2 * lax.rem(so, 16) + so // 16).astype(F32)
    kxy = mm(jnp.concatenate([kx, ky, jnp.zeros((6, STK), F32)], axis=0), perm)

    acc_re = jnp.zeros((16, 128), F32)
    acc_im = jnp.zeros((16, 128), F32)
    for r in range(16):
        lanes = slice(128 * r, 128 * (r + 1))
        p_re, p_im = proj[0, :, lanes], proj[1, :, lanes]
        a, b = m_re[r : r + 1, :], m_im[r : r + 1, :]
        acc_re += a * p_re + b * p_im
        acc_im += b * p_re - a * p_im
    ones = jnp.ones((8, 128), F32)
    part = mm(ones, jnp.concatenate([acc_re, acc_im], axis=0), NT, HIGHEST)

    field = cosp * d1 + sinp * d2
    place = lax.rem(lax.broadcasted_iota(jnp.int32, (256, STK), 0), 8)
    field = jnp.where(
        place == 6,
        jnp.broadcast_to(kxy[0:1, :], (256, STK)),
        jnp.where(place == 7, jnp.broadcast_to(kxy[1:2, :], (256, STK)), field[:, :STK]),
    )
    message = jnp.concatenate(
        [field, jnp.broadcast_to(part[0:1, :], (256, STK)), jnp.zeros((256, 64), F32)], axis=1
    )
    mine[0] = message.reshape(NF, 8, 128)
    for b in range(1, 4):
        mine[b] = pltpu.roll(message, 32 * b, 1).reshape(NF, 8, 128)
    got[0] = mine[0, me]

    pl.semaphore_wait(barrier, NF - 1 + 7 + 1)

    def send_field(k, _):
        to = lax.rem(me + k, NF)
        pltpu.make_async_remote_copy(
            mine.at[lax.rem(k, 4), to], got.at[k], sa, ra, device_id={"fft": to}, device_id_type=MESH
        ).start()
        return 0

    lax.fori_loop(1, NF, send_field, 0)

    def send_slab(k, _):
        to = lax.rem(band + 2 * k, 16)
        pltpu.make_async_remote_copy(
            pool.at[core, row], pool.at[core, row], ss, rs, device_id={"band": to}, device_id_type=MESH
        ).start()
        return 0

    lax.fori_loop(1, 8, send_slab, 0)

    sr_i = lax.broadcasted_iota(jnp.int32, (16, STK), 1) // 2
    rr_i = lax.broadcasted_iota(jnp.int32, (16, STK), 0)
    s_i = lax.broadcasted_iota(jnp.int32, (STK, 128), 0)
    l_i = lax.broadcasted_iota(jnp.int32, (STK, 128), 1)
    half = (lax.rem(s_i, 2) == l_i // GZ).astype(F32)
    kx16 = mm(jnp.where(sr_i == rr_i, jnp.broadcast_to(kx, (16, STK)), 0.0), half) - RADIUS
    ky16 = mm(jnp.where(sr_i == rr_i, jnp.broadcast_to(ky, (16, STK)), 0.0), half) - RADIUS
    fz = jnp.where(dep16 < NZ // 2, dep16, dep16 - NZ).astype(F32)
    kin = (0.5 / (RADIUS * RADIUS)) * (kx16 * kx16 + ky16 * ky16 + fz * fz)

    dfull = jnp.zeros((16, 16), F32)
    p_i = lax.broadcasted_iota(jnp.int32, (16, 8), 0)
    for a in range(2):
        owner = (p_i == jnp.broadcast_to(atoms[a : a + 1, :], (16, 8))).astype(F32)
        dfull += mm(mm(owner, coup[a], NN, HIGHEST), owner, NT, HIGHEST)

    whole = pltpu.make_async_remote_copy(
        got.at[pl.ds(1, NF - 1)], got.at[pl.ds(1, NF - 1)], sa, ra, device_id={"fft": lax.rem(me + 1, NF)}, device_id_type=MESH
    )
    whole.wait_recv()
    lane = lax.broadcasted_iota(jnp.int32, (8, 128), 1) // 32
    sticks = []
    others = []
    for a in range(8):
        tile = jnp.zeros((8, 128), F32)
        for b in range(4):
            tile = jnp.where(lane == b, got[4 * a + b], tile)
        sticks.append(tile)
    total = jnp.zeros((8, 128), F32)
    for b in range(4):
        piece = jnp.zeros((8, 128), F32)
        for a in range(8):
            piece += got[4 * a + b]
        piece = jnp.where(lane == (b + 1) % 4, piece, 0.0)
        shift = (128 - 32 * (b + 1)) % 128
        total += pltpu.roll(piece, shift, 1) if shift else piece
    pr, pi = total[0:1, 0:16], total[0:1, 16:32]
    c_re = jnp.sum(dfull * pr, axis=1, keepdims=True)
    c_im = jnp.sum(dfull * pi, axis=1, keepdims=True)
    for r in range(16):
        lanes = slice(128 * r, 128 * (r + 1))
        p_re, p_im = proj[0, :, lanes], proj[1, :, lanes]
        nonl[0, r : r + 1, :] = jnp.sum(c_re * p_re - c_im * p_im, axis=0, keepdims=True)
        nonl[1, r : r + 1, :] = jnp.sum(c_re * p_im + c_im * p_re, axis=0, keepdims=True)

    ix = lax.broadcasted_iota(jnp.int32, (KX, 128), 0).astype(F32)
    iy = lax.broadcasted_iota(jnp.int32, (KY, 128), 0).astype(F32)
    grid = jnp.zeros((6 * KX, KY), F32)
    hot_y = []
    for a in range(8):
        tile = sticks[a]
        hot_y.append((iy == tile[7:8, :]).astype(F32).astype(BF16))
        on = ix == tile[6:7, :]
        hi = tile.astype(BF16).astype(F32)
        lo = tile - hi
        z_hi = jnp.concatenate([jnp.where(on, hi[p : p + 1, :], 0.0) for p in range(6)], axis=0)
        z_lo = jnp.concatenate([jnp.where(on, lo[p : p + 1, :], 0.0) for p in range(6)], axis=0)
        grid += mm(z_hi.astype(BF16), hot_y[a], NT, None) + mm(z_lo.astype(BF16), hot_y[a], NT, None)

    left = jnp.concatenate(
        [jnp.concatenate([grid[2 * z * KX : (2 * z + 1) * KX], grid[(2 * z + 1) * KX : (2 * z + 2) * KX]], axis=1) for z in range(PLANES)],
        axis=0,
    )
    inv_y = mm(left, wiy[...])
    fields = []
    for z in range(PLANES):
        rows = inv_y[z * KX : (z + 1) * KX]
        right = jnp.concatenate([rows[:, :V], rows[:, V:]], axis=0)
        grid_z = mm(wix[...], right)
        fields.append(jnp.concatenate([grid_z[:U] * pot[z], grid_z[U:] * pot[z]], axis=1))
    fwd_y = mm(jnp.concatenate(fields, axis=0), wfy[...])
    right = jnp.concatenate(
        [
            jnp.concatenate([fwd_y[z * U : (z + 1) * U, :KY], fwd_y[z * U : (z + 1) * U, KY:]], axis=0)
            for z in range(PLANES)
        ],
        axis=1,
    )
    back = mm(wfx[...], right)
    stack = jnp.concatenate(
        [back[c * KX : (c + 1) * KX, z * KY : (z + 1) * KY] for z in range(PLANES) for c in range(2)], axis=0
    )
    hi = stack.astype(BF16)
    lo = (stack - hi.astype(F32)).astype(BF16)
    both = jnp.concatenate([hi, lo], axis=1)
    for a in range(8):
        spread = mm(both, jnp.concatenate([hot_y[a], hot_y[a]], axis=0), NN, None)
        on = ix == sticks[a][6:7, :]
        rows = [
            jnp.sum(jnp.where(on, spread[p * KX : (p + 1) * KX], 0.0), axis=0, keepdims=True) for p in range(6)
        ]
        tile = jnp.concatenate(rows + [jnp.zeros((2, 128), F32)], axis=0)
        tiles[0, a] = tile
        for b in range(1, 4):
            tiles[b, a] = pltpu.roll(tile, 128 - 32 * b, 1)
    ret[me] = tiles[0, 0]

    def send_back(k, _):
        to = lax.rem(me + NF - k, NF)
        pltpu.make_async_remote_copy(
            tiles.at[lax.rem(k, 4), k // 4], ret.at[me], sb, rb, device_id={"fft": to}, device_id_type=MESH
        ).start()
        return 0

    lax.fori_loop(1, NF, send_back, 0)

    seven = pltpu.make_async_remote_copy(
        pool.at[0, pl.ds(0, 7)], pool.at[0, pl.ds(0, 7)], ss, rs, device_id={"band": twin}, device_id_type=MESH
    )
    seven.wait_recv()
    swap = pltpu.make_async_remote_copy(
        pool.at[core], pool.at[core], sf, rf, device_id={"band": twin}, device_id_type=MESH
    )
    swap.start()

    sign = jnp.where(lax.broadcasted_iota(jnp.int32, (8, 128), 0) < 4, 1.0, -1.0)

    def correlate(v_re, v_im, source):
        def step(k, _):
            u = jnp.zeros((8, 128), F32)
            w = jnp.zeros((8, 128), F32)
            for r in range(16):
                block = pool[lax.rem(k, 2), k // 2, :, 128 * r : 128 * (r + 1)]
                u += block * v_re[r : r + 1, :]
                w += block * v_im[r : r + 1, :]
            w = jnp.concatenate([w[4:8], w[0:4]], axis=0)
            source[k] = w + u * sign
            return 0

        lax.fori_loop(0, 16, step, 0)
        sums = mm(ones, source[...].reshape(128, 128), NT, HIGHEST)
        return sums[0:1, :]

    swap.wait_recv()
    s_row = correlate(m_re, m_im, work)

    every = pltpu.make_async_remote_copy(
        got.at[pl.ds(1, NF - 1)], ret.at[pl.ds(0, NF - 1)], sb, rb, device_id={"fft": lax.rem(me + 1, NF)}, device_id_type=MESH
    )
    every.wait_recv()
    came = ret[...].reshape(256, 128)
    ab = jnp.concatenate([came * cosp, came * sinp], axis=0)
    loc = mm(tback[...], ab).T
    loc_re = jnp.concatenate([loc[0:16, :GZ], loc[16:32, :GZ]], axis=1)
    loc_im = jnp.concatenate([loc[0:16, GZ:], loc[16:32, GZ:]], axis=1)
    a_re = jnp.where(mask, kin * m_re + loc_re + nonl[0], 0.0)
    a_im = jnp.where(mask, kin * m_im + loc_im + nonl[1], 0.0)
    out[0] = a_re
    out[1] = a_im
    h_row = correlate(a_re, a_im, work)
    red[me] = jnp.concatenate([h_row, s_row], axis=0)

    def send_sum(k, _):
        pltpu.make_async_remote_copy(
            red.at[me], red.at[me], sr, rr, device_id={"fft": lax.rem(me + k, NF)}, device_id_type=MESH
        ).start()
        return 0

    lax.fori_loop(1, NF, send_sum, 0)
    last = pltpu.make_async_remote_copy(
        red.at[pl.ds(0, NF - 1)], red.at[pl.ds(0, NF - 1)], sr, rr, device_id={"fft": lax.rem(me + 1, NF)}, device_id_type=MESH
    )
    last.wait_recv()
    both_rows = jnp.sum(red[...], axis=0)
    li = lax.broadcasted_iota(jnp.int32, (128, 128), 0)
    lo_ = lax.broadcasted_iota(jnp.int32, (128, 128), 1)
    want = (lax.rem(lo_, 64) // 4) * 8 + (lo_ // 64) * 4 + lax.rem(lo_, 4)
    order = (li == want).astype(F32)
    final = mm(jnp.concatenate([both_rows, jnp.zeros((6, 128), F32)], axis=0), order, NN, HIGHEST)
    out_h[0] = final[0:1, 0:64]
    out_h[1] = final[0:1, 64:128]
    out_s[0] = final[1:2, 0:64]
    out_s[1] = final[1:2, 64:128]

    whole.wait_send()
    seven.wait_send()
    swap.wait_send()
    every.wait_send()
    last.wait_send()


def shards(orbitals, stick_columns, stick_depths, potential, projectors, atom_projectors, couplings, slab_orbitals):
    pot = jnp.pad(potential.reshape(PLANES, NX, NY), ((0, 0), (0, U - NX), (0, V - NY)))
    args = (
        orbitals.reshape(2, 16, 128),
        stick_columns.reshape(1, STK),
        stick_depths,
        pot,
        projectors,
        atom_projectors,
        couplings,
        slab_orbitals,
    ) + tuple(jnp.asarray(t) for t in tables())
    vmem = pl.BlockSpec(memory_space=pltpu.VMEM)
    dma = pltpu.SemaphoreType.DMA
    applied, proj_h, proj_s = pl.pallas_call(
        kernel,
        out_shape=(
            jax.ShapeDtypeStruct((2, 16, 128), F32),
            jax.ShapeDtypeStruct((2, 1, 64), F32),
            jax.ShapeDtypeStruct((2, 1, 64), F32),
        ),
        in_specs=[vmem] * len(args),
        out_specs=(vmem, vmem, vmem),
        scratch_shapes=[
            pltpu.VMEM((4, NF, 8, 128), F32),
            pltpu.VMEM((NF, 8, 128), F32),
            pltpu.VMEM((4, 8, 8, 128), F32),
            pltpu.VMEM((NF, 8, 128), F32),
            pltpu.VMEM((2, 8, 8, 2048), F32),
            pltpu.VMEM((NF, 2, 128), F32),
            pltpu.VMEM((16, 8, 128), F32),
            pltpu.VMEM((2, 16, 128), F32),
            pltpu.VMEM((8, 128), F32),
        ]
        + [dma] * 10,
        compiler_params=pltpu.CompilerParams(
            collective_id=0, has_side_effects=True, vmem_limit_bytes=48 * 1024 * 1024
        ),
        name="davidson",
    )(*args)
    return applied.reshape(2, 1, 2048), proj_h, proj_s


def solution(mesh):
    in_specs = (
        P(None, "band", "fft"),
        P("fft"),
        P("fft", None),
        P("fft", None),
        P(None, None, "fft"),
        P(),
        P(),
        P(None, "band", "fft"),
    )
    out_specs = (P(None, "band", "fft"), P(None, "band", None), P(None, "band", None))
    return jax.shard_map(shards, mesh=mesh, in_specs=in_specs, out_specs=out_specs, check_vma=False)
```

time: 437 us -> 48.6 us (0.11)
  the two profiles are of different devices: /device:TPU:48 before, /device:TPU:1 now
where the time goes in v1:
time: 48.6 us; the launch traced here: 48.3 us
  Pallas kernels  40 us (82%)
  local copies, waits for them, and re-layouts  7.5 us (15%)
  between operations  0.81 us (2%)
    pallas_call x1, Pallas kernels, shards(): pl.pallas_call(kernel, out_shape=(jax.ShapeDtypeStruct((2, 16, 128), F32)...  40 us
    unnamed x33, local copies, waits for them, and re-layouts  5.61 us
    reshape x1, local copies, waits for them, and re-layouts, shards(): potential.reshape(PLANES, NX, NY)  1.84 us

profile of v1, /device:TPU:1, one launch (start us, length us, event | category | flops | bytes accessed | tf_op | source)
XLA Modules:
  0.0 48.3 jit_solution(1739820548655911691)
XLA Ops:
  0.6 0.0 copy-start.2
  0.6 0.0 copy-start.3
  0.7 0.0 copy-start.4
  0.7 0.0 copy-start.7
  0.7 0.0 copy-start.13
  0.7 1.8 %reshape.20 = f32[3,180,180]{2,1,0:T(8,128)S(1)} reshape(f32[3,32400]{1,0:T(4,128)} %param.19) | data formatting | bytes 777600 | tf_op jit(solution)/shard_map/reshape | solution.py:390
  2.5 0.0 copy-start
  2.5 0.0 copy-start.1
  2.6 0.0 copy-start.9
  2.6 0.0 copy-start.10
  2.6 0.0 copy-start.11
  2.6 0.0 copy-start.12
  2.6 0.0 copy-start.14
  2.7 0.0 copy-done.2
  2.7 0.0 copy-done.3
  2.7 0.0 copy-done.4
  2.7 0.0 copy-done.7
  2.7 0.0 copy-done.13
  2.7 0.9 %copy-done = f32[512,256]{1,0:T(8,128)S(1)} copy-done((f32[512,256]{1,0:T(8,128)S(1)}, f32[512,256]{1,0:T(8,128)}, u32[]{:S(2)}) %copy-start) | copy-done | bytes 524312
  3.6 0.2 copy-done.1
  3.7 0.0 copy-done.9
  3.7 0.0 copy-done.10
  3.7 0.0 copy-done.11
  3.8 0.0 copy-done.12
  3.8 0.0 copy-done.14
  3.8 0.0 copy-start.5
  3.8 0.9 %copy-done.5 = f32[128,512]{1,0:T(8,128)S(1)} copy-done((f32[128,512]{1,0:T(8,128)S(1)}, f32[128,512]{1,0:T(8,128)}, u32[]{:S(2)}) %copy-start.5) | copy-done | bytes 262168
  4.7 0.0 copy-start.6
  4.7 0.9 %copy-done.6 = f32[2,256,128]{2,1,0:T(8,128)S(1)} copy-done((f32[2,256,128]{2,1,0:T(8,128)S(1)}, f32[2,256,128]{2,1,0:T(8,128)}, u32[]{:S(2)}) %copy-start.6) | copy-done | bytes 262168
  5.7 0.0 copy-start.8
  5.7 0.9 %copy-done.8 = f32[256,128]{1,0:T(8,128)S(1)} copy-done((f32[256,128]{1,0:T(8,128)S(1)}, f32[256,128]{1,0:T(8,128)}, u32[]{:S(2)}) %copy-start.8) | copy-done | bytes 131096
  6.6 40.0 %davidson.1 = (f32[2,16,128]{2,1,0:T(8,128)S(1)}, f32[2,1,64]{2,1,0:T(1,128)S(1)}, f32[2,1,64]{2,1,0:T(1,128)S(1)}) custom-call(f32[2,16,128]{2,1,0:T(8,128)S(1)} %bitcast.3, s32[1,32]{1,0:T(1,128)S(1)} %bitcast.5, s32[32,64]{1,0:T(8,128)S(1)} %copy-done.11, f32[3,192,256]{2,1,0:T(8,128)S(1)} %pad.4.pot, f32[2,16,2048]{2,1,0:T(8,128)S(1)} %copy-done.4, ...), custom_call_target="tpu_custom_call" | custom-call | tf_op jit(solution)/shard_map/davidson/pallas_call | solution.py:403
  46.6 0.6 %copy.23 = f32[2,1,2048]{2,1,0:T(1,128)} copy(f32[2,1,2048]{2,1,0:T(1,128)S(1)} %bitcast.4) | data formatting | bytes 32768
  47.2 0.6 %copy.24 = f32[2,1,64]{2,1,0:T(1,128)} copy(f32[2,1,64]{2,1,0:T(1,128)S(1)} %get-tuple-element.16) | data formatting | bytes 1024
  47.7 0.6 %copy.25 = f32[2,1,64]{2,1,0:T(1,128)} copy(f32[2,1,64]{2,1,0:T(1,128)S(1)} %get-tuple-element.17) | data formatting | bytes 1024
  (1 shorter events, 0.0 us)
Async XLA Ops:
  0.6 2.0 %copy-start.2 = (f32[384,192]{1,0:T(8,128)S(1)}, f32[384,192]{1,0:T(8,128)}, u32[]{:S(2)}) copy-start(f32[384,192]{1,0:T(8,128)} %constant.23.clone.wix) | copy-start | bytes 884740
  0.6 2.0 %copy-start.3 = (f32[192,384]{1,0:T(8,128)S(1)}, f32[192,384]{1,0:T(8,128)}, u32[]{:S(2)}) copy-start(f32[192,384]{1,0:T(8,128)} %constant.25.clone.wfx) | copy-start | bytes 884740
  0.7 2.0 %copy-start.4 = (f32[2,16,2048]{2,1,0:T(8,128)S(1)}, f32[2,16,2048]{2,1,0:T(8,128)}, u32[]{:S(2)}) copy-start(f32[2,16,2048]{2,1,0:T(8,128)} %proj.1) | copy-start | bytes 786436
  0.7 2.0 %copy-start.7 = (f32[256,128]{1,0:T(8,128)S(1)}, f32[256,128]{1,0:T(8,128)}, u32[]{:S(2)}) copy-start(f32[256,128]{1,0:T(8,128)} %constant.20.clone.t2) | copy-start | bytes 393220
  0.7 2.0 %copy-start.13 = (s32[2,8]{1,0:T(2,128)S(1)}, s32[2,8]{1,0:T(2,128)}, u32[]{:S(2)}) copy-start(s32[2,8]{1,0:T(2,128)} %atoms.1) | copy-start | bytes 196
  2.5 1.0 %copy-start = (f32[512,256]{1,0:T(8,128)S(1)}, f32[512,256]{1,0:T(8,128)}, u32[]{:S(2)}) copy-start(f32[512,256]{1,0:T(8,128)} %constant.24.clone.wfy) | copy-start | bytes 1572868
  2.5 1.2 %copy-start.1 = (f32[256,512]{1,0:T(8,128)S(1)}, f32[256,512]{1,0:T(8,128)}, u32[]{:S(2)}) copy-start(f32[256,512]{1,0:T(8,128)} %constant.22.clone.wiy) | copy-start | bytes 1572868
  2.6 1.2 %copy-start.9 = (f32[2,4,2048]{2,1,0:T(4,128)S(1)}, f32[2,4,2048]{2,1,0:T(4,128)}, u32[]{:S(2)}) copy-start(f32[2,4,2048]{2,1,0:T(4,128)} %slab.1) | copy-start | bytes 196612
  2.6 1.2 %copy-start.10 = (f32[2,1,2048]{2,1,0:T(1,128)S(1)}, f32[2,1,2048]{2,1,0:T(1,128)}, u32[]{:S(2)}) copy-start(f32[2,1,2048]{2,1,0:T(1,128)} %param.16) | copy-start | bytes 49156
  2.6 1.2 %copy-start.11 = (s32[32,64]{1,0:T(8,128)S(1)}, s32[32,64]{1,0:T(8,128)}, u32[]{:S(2)}) copy-start(s32[32,64]{1,0:T(8,128)} %deps.1) | copy-start | bytes 24580
  2.6 1.2 %copy-start.12 = (f32[2,8,8]{2,1,0:T(8,128)S(1)}, f32[2,8,8]{2,1,0:T(8,128)}, u32[]{:S(2)}) copy-start(f32[2,8,8]{2,1,0:T(8,128)} %coup.1) | copy-start | bytes 1540
  2.6 1.1 %copy-start.14 = (s32[32]{0:T(128)S(1)}, s32[32]{0:T(128)}, u32[]{:S(2)}) copy-start(s32[32]{0:T(128)} %param.17) | copy-start | bytes 388
  3.8 1.0 %copy-start.5 = (f32[128,512]{1,0:T(8,128)S(1)}, f32[128,512]{1,0:T(8,128)}, u32[]{:S(2)}) copy-start(f32[128,512]{1,0:T(8,128)} %constant.26.clone.tback) | copy-start | bytes 786436
  4.7 0.9 %copy-start.6 = (f32[2,256,128]{2,1,0:T(8,128)S(1)}, f32[2,256,128]{2,1,0:T(8,128)}, u32[]{:S(2)}) copy-start(f32[2,256,128]{2,1,0:T(8,128)} %constant.21.clone.turn) | copy-start | bytes 786436
  5.7 0.9 %copy-start.8 = (f32[256,128]{1,0:T(8,128)S(1)}, f32[256,128]{1,0:T(8,128)}, u32[]{:S(2)}) copy-start(f32[256,128]{1,0:T(8,128)} %constant.19.clone.t1) | copy-start | bytes 393220

commit v2 on v1

v2 whole, which is shorter than its diff:
```python
import functools
import math

import jax
import jax.numpy as jnp
import ml_dtypes
import numpy as np
from jax import lax
from jax.experimental import pallas as pl
from jax.experimental.pallas import tpu as pltpu
from jax.sharding import PartitionSpec as P

NX = 180
NY = 180
NZ = 96
GZ = 64
RADIUS = 45
NXY = NX * NY
NF = 32
STK = 32
KX = 96
KY = 128
U = 192
V = 256
PLANES = 3

MESH = pl.DeviceIdType.MESH
HIGHEST = lax.Precision.HIGHEST
F32 = jnp.float32
BF16 = jnp.bfloat16
NN = (((1,), (0,)), ((), ()))
NT = (((1,), (1,)), ((), ()))


def mm(a, b, dims=NN, precision=None):
    return lax.dot_general(a, b, dims, precision=precision, preferred_element_type=F32)


def split(x):
    hi = x.astype(BF16)
    return hi, (x - hi.astype(F32)).astype(BF16)


def mm_right(a, table, dims=NN):
    hi, lo = split(a)
    return mm(hi, table[0], dims) + (mm(lo, table[0], dims) + mm(hi, table[1], dims))


def mm_left(table, b, dims=NN):
    hi, lo = split(b)
    return mm(table[0], hi, dims) + (mm(table[0], lo, dims) + mm(table[1], hi, dims))


def far_first():
    hops = lambda o: min(o[0], 8 - o[0]) + min(o[1], 4 - o[1])
    every = [(dz, dx) for dz in range(8) for dx in range(4)]
    return sorted((o for o in every if o != (0, 0)), key=lambda o: (-hops(o), o))


OFFSETS = far_first()


@functools.lru_cache(maxsize=None)
def tables():
    tau = 2.0 * math.pi
    j = np.arange(GZ)
    depth = np.arange(NZ + 1)
    t1 = np.zeros((4, NF, 2, 2, GZ))
    t2 = np.zeros((4, NF, 2, 2, GZ))
    tb = np.zeros((2, GZ, 2, 4, NF, 2))
    turn = np.zeros((2, 4, NF, 2, 128))
    for d in range(NF):
        for p in range(2 * PLANES):
            h, q = p // 4, p % 4
            z = PLANES * d + p // 2
            th = tau * (j * z % NZ) / NZ
            c, s = np.cos(th), np.sin(th)
            if p % 2 == 0:
                t1[q, d, h] = c, -s
                t2[q, d, h] = -s, -c
                tb[0, :, 0, q, d, h], tb[0, :, 1, q, d, h] = c, -s
                tb[1, :, 0, q, d, h], tb[1, :, 1, q, d, h] = -s, -c
            else:
                t1[q, d, h] = s, c
                t2[q, d, h] = c, -s
                tb[0, :, 0, q, d, h], tb[0, :, 1, q, d, h] = s, c
                tb[1, :, 0, q, d, h], tb[1, :, 1, q, d, h] = c, -s
            ph = tau * (depth * z % NZ) / NZ
            turn[0, q, d, h, : NZ + 1] = np.cos(ph)
            turn[1, q, d, h, : NZ + 1] = np.sin(ph)
    n = 2 * RADIUS + 1
    k = np.arange(n) - RADIUS
    g = np.arange(NX)
    ang = tau * ((k[:, None] * g[None, :]) % NX) / NX
    c, s = np.cos(ang), np.sin(ang)
    wiy = np.zeros((2, KY, 2, V))
    wiy[0, :n, 0, :NY], wiy[0, :n, 1, :NY] = c / NY, s / NY
    wiy[1, :n, 0, :NY], wiy[1, :n, 1, :NY] = -s / NY, c / NY
    wix = np.zeros((2, U, 2, KX))
    wix[0, :NX, 0, :n], wix[0, :NX, 1, :n] = c.T / NX, -s.T / NX
    wix[1, :NX, 0, :n], wix[1, :NX, 1, :n] = s.T / NX, c.T / NX
    wfy = np.zeros((2, V, 2, KY))
    wfy[0, :NY, 0, :n], wfy[0, :NY, 1, :n] = c.T, -s.T
    wfy[1, :NY, 0, :n], wfy[1, :NY, 1, :n] = s.T, c.T
    wfx = np.zeros((2, KX, 2, U))
    wfx[0, :n, 0, :NX], wfx[0, :n, 1, :NX] = c, s
    wfx[1, :n, 0, :NX], wfx[1, :n, 1, :NX] = -s, c
    back = np.transpose(tb.reshape(2, GZ, 2, 256), (2, 1, 0, 3)).reshape(2 * GZ, 512)
    tz = np.concatenate([t1.reshape(256, 128), t2.reshape(256, 128)], axis=0) / NZ

    def parts(x):
        x = np.asarray(x, np.float32)
        hi = x.astype(ml_dtypes.bfloat16)
        lo = (x - hi.astype(np.float32)).astype(ml_dtypes.bfloat16)
        return np.stack([hi, lo])

    return (
        parts(tz),
        parts(turn.reshape(512, 128)),
        parts(wiy.reshape(2 * KY, 2 * V)),
        parts(wix.reshape(2 * U, 2 * KX)),
        parts(wfy.reshape(2 * V, 2 * KY)),
        parts(wfx.reshape(2 * KX, 2 * U)),
        parts(back),
    )


def kernel(
    orb_h, cols_h, deps_h, pot_h, proj_h, atoms_h, coup_h, slab_h, tz_h, turn_h, wiy_h, wix_h, wfy_h, wfx_h, tback_h,
    out, out_sums,
    orb, cols, deps, pot, proj, atoms, coup, slab, tz, turn, wiy, wix, wfy, wfx, tback,
    mine, got, tiles, ret, pool, red, nonl, vecs, field_pot,
    loads, sa, ra, sb, rb, near_s, near_r, far_s, far_r, sf, rf, sr, rr,
):
    me = lax.axis_index("fft")
    band = lax.axis_index("band")
    my_z, my_x = me // 4, lax.rem(me, 4)
    core = lax.rem(band, 2)
    row = band // 2
    twin = band + 1 - 2 * core

    def fft_at(dz, dx):
        return lax.rem(my_z + dz, 8) * 4 + lax.rem(my_x + dx, 4)

    def band_at(dy):
        return lax.rem(band + 2 * dy, 16)

    barrier = pltpu.get_barrier_semaphore()
    for dz, dx in OFFSETS:
        pl.semaphore_signal(barrier, inc=1, device_id={"fft": fft_at(dz, dx)}, device_id_type=MESH)
    for dy in (2, 6, 1, 7):
        pl.semaphore_signal(barrier, inc=1, device_id={"band": band_at(dy)}, device_id_type=MESH)
    pl.semaphore_signal(barrier, inc=1, device_id={"band": twin}, device_id_type=MESH)

    pairs = (
        (orb_h, orb), (deps_h, deps), (cols_h, cols), (tz_h, tz), (turn_h, turn), (proj_h, proj), (slab_h, slab),
        (pot_h, pot), (atoms_h, atoms), (coup_h, coup), (wiy_h, wiy), (wix_h, wix), (wfy_h, wfy), (wfx_h, wfx),
        (tback_h, tback),
    )
    copies = [pltpu.make_async_copy(a, b, loads.at[i]) for i, (a, b) in enumerate(pairs)]
    for c in copies:
        c.start()
    for c in copies[:5]:
        c.wait()

    dep_even = deps[pl.ds(0, 16, stride=2), :]
    dep_odd = deps[pl.ds(1, 16, stride=2), :]
    dep16 = jnp.concatenate([dep_even, dep_odd], axis=1)
    mask = dep16 < NZ
    m_re = jnp.where(mask, orb[0], 0.0)
    m_im = jnp.where(mask, orb[1], 0.0)
    x2 = jnp.concatenate(
        [
            jnp.concatenate([m_re[:, :GZ], m_im[:, :GZ]], axis=1),
            jnp.concatenate([m_re[:, GZ:], m_im[:, GZ:]], axis=1),
        ],
        axis=0,
    )
    x2 = jnp.concatenate([x2] * 4, axis=0)
    d12 = mm_left(tz, x2, NT)

    dep32 = jnp.concatenate([dep_even, dep_odd] * 4, axis=0).astype(F32)
    first = (lax.broadcasted_iota(jnp.int32, (8, GZ), 1) == 0).astype(F32)
    dep0 = mm(first, dep32, NT)
    hot = (lax.broadcasted_iota(jnp.int32, (128, 128), 0).astype(F32) == dep0[0:1, :]).astype(F32).astype(BF16)
    phase = mm(turn[0], hot) + mm(turn[1], hot)
    cosp, sinp = phase[:256], phase[256:]

    colf = cols[...].astype(F32)
    qx = jnp.floor((colf + 0.5) * (1.0 / NY))
    qy = colf - NY * qx
    live = cols[...] < NXY
    kx = jnp.where(live, jnp.where(qx < 90.0, qx, qx - NX) + (RADIUS + 1), 0.0)
    ky = jnp.where(live, jnp.where(qy < 90.0, qy, qy - NY) + (RADIUS + 1), 0.0)
    si = lax.broadcasted_iota(jnp.int32, (STK, 128), 0)
    so = lax.rem(lax.broadcasted_iota(jnp.int32, (STK, 128), 1), 32)
    perm = (si == 2 * lax.rem(so, 16) + so // 16).astype(F32)
    kxy = mm(jnp.concatenate([kx, ky, jnp.zeros((6, STK), F32)], axis=0), perm)
    code = kxy[0:1, :] * 128.0 + kxy[1:2, :]

    copies[5].wait()
    acc_re = jnp.zeros((16, 128), F32)
    acc_im = jnp.zeros((16, 128), F32)
    for r in range(16):
        lanes = slice(128 * r, 128 * (r + 1))
        p_re, p_im = proj[0, :, lanes], proj[1, :, lanes]
        a, b = m_re[r : r + 1, :], m_im[r : r + 1, :]
        acc_re += a * p_re + b * p_im
        acc_im += b * p_re - a * p_im
    ones = jnp.ones((8, 128), F32)
    part = mm(ones, jnp.concatenate([acc_re, acc_im] * 4, axis=0), NT, HIGHEST)

    field = cosp * d12[:256] + sinp * d12[256:]
    group = lax.broadcasted_iota(jnp.int32, (64, 128), 1) // 32
    odd = lax.rem(lax.broadcasted_iota(jnp.int32, (64, 128), 0), 2) == 1
    message = jnp.where(
        group == 0,
        field[0:64],
        jnp.where(
            group == 1,
            field[64:128],
            jnp.where(
                group == 2,
                jnp.where(odd, jnp.broadcast_to(code, (64, 128)), field[128:192]),
                jnp.where(odd, jnp.broadcast_to(part[0:1, :], (64, 128)), field[192:256]),
            ),
        ),
    )
    for d in range(NF):
        mine[d] = message[2 * d : 2 * d + 2]
    got[0] = mine[me]

    copies[6].wait()
    pool[core, row] = jnp.concatenate([slab[0], slab[1]], axis=0)

    pl.semaphore_wait(barrier, NF - 1 + 4 + 1)

    for dz, dx in OFFSETS:
        to = fft_at(dz, dx)
        pltpu.make_async_remote_copy(
            mine.at[to], got.at[4 * dz + dx], sa, ra, device_id={"fft": to}, device_id_type=MESH
        ).start()

    def to_band(src, dst, send, recv, dy):
        return pltpu.make_async_remote_copy(
            src, dst, send, recv, device_id={"band": band_at(dy)}, device_id_type=MESH
        )

    own = pool.at[core, row]
    near = [to_band(own, own, near_s.at[i], near_r.at[i], dy) for i, dy in enumerate((2, 6, 1, 7))]
    for c in near:
        c.start()

    sr_i = lax.broadcasted_iota(jnp.int32, (16, STK), 1) // 2
    rr_i = lax.broadcasted_iota(jnp.int32, (16, STK), 0)
    s_i = lax.broadcasted_iota(jnp.int32, (STK, 128), 0)
    l_i = lax.broadcasted_iota(jnp.int32, (STK, 128), 1)
    half = (lax.rem(s_i, 2) == l_i // GZ).astype(F32)
    kx16 = mm(jnp.where(sr_i == rr_i, jnp.broadcast_to(kx, (16, STK)), 0.0), half) - (RADIUS + 1)
    ky16 = mm(jnp.where(sr_i == rr_i, jnp.broadcast_to(ky, (16, STK)), 0.0), half) - (RADIUS + 1)
    fz = jnp.where(dep16 < NZ // 2, dep16, dep16 - NZ).astype(F32)
    kin = (0.5 / (RADIUS * RADIUS)) * (kx16 * kx16 + ky16 * ky16 + fz * fz)

    for c in copies[7:]:
        c.wait()

    dfull = jnp.zeros((16, 16), F32)
    p_i = lax.broadcasted_iota(jnp.int32, (16, 8), 0)
    for a in range(2):
        owner = (p_i == jnp.broadcast_to(atoms[a : a + 1, :], (16, 8))).astype(F32)
        dfull += mm(mm(owner, coup[a], NN, HIGHEST), owner, NT, HIGHEST)

    field_pot[...] = jnp.zeros_like(field_pot)
    for x in range(NX):
        field_pot[0, 4 * x : 4 * x + PLANES, :] = pot[:, NY * x : NY * x + 128]
        field_pot[1, 4 * x : 4 * x + PLANES, 0 : NY - 128] = pot[:, NY * x + 128 : NY * x + NY]

    ahead = pool.at[core, lax.rem(row + 6, 8)]
    behind = pool.at[core, lax.rem(row + 2, 8)]
    first_half, second_half = pl.ds(0, 1024), pl.ds(1024, 1024)
    far = (
        to_band(ahead, ahead, far_s.at[0], far_r.at[0], 1),
        to_band(ahead.at[:, first_half], ahead.at[:, first_half], far_s.at[1], far_r.at[1], 2),
        to_band(behind, behind, far_s.at[2], far_r.at[2], 7),
        to_band(behind.at[:, second_half], behind.at[:, second_half], far_s.at[3], far_r.at[3], 6),
    )

    whole = pltpu.make_async_remote_copy(
        got.at[pl.ds(1, NF - 1)], got.at[pl.ds(1, NF - 1)], sa, ra, device_id={"fft": fft_at(0, 1)}, device_id_type=MESH
    )
    whole.wait_recv()
    near[0].wait_recv()
    far[0].start()
    far[1].start()
    near[1].wait_recv()
    far[2].start()
    far[3].start()

    lane = lax.broadcasted_iota(jnp.int32, (8, 128), 1) // 32
    parts = [[None] * 4 for _ in range(2)]
    for h in range(2):
        for b in range(4):
            rows = jnp.concatenate([got[4 * a + b, h : h + 1, :] for a in range(8)], axis=0)
            for q in range(4):
                shift = 32 * ((b - q) % 4)
                turned = pltpu.roll(rows, shift, 1) if shift else rows
                parts[h][q] = turned if b == 0 else jnp.where(lane == b, turned, parts[h][q])
    fields = [parts[p // 4][p % 4] for p in range(6)]
    code = parts[1][2]
    kx_at = jnp.floor(code * (1.0 / 128.0))
    ky_at = code - 128.0 * kx_at
    kx_at -= 1.0
    ky_at -= 1.0

    ix = lax.broadcasted_iota(jnp.int32, (KX, 128), 0).astype(F32)
    iy = lax.broadcasted_iota(jnp.int32, (KY, 128), 0).astype(F32)
    his = [f.astype(BF16).astype(F32) for f in fields]
    los = [f - h for f, h in zip(fields, his)]
    on = [ix == kx_at[a : a + 1, :] for a in range(8)]
    hot_y = [(iy == ky_at[a : a + 1, :]).astype(F32).astype(BF16) for a in range(8)]
    grid = jnp.zeros((6 * KX, KY), F32)
    for a in range(0, 8, 2):
        wide = jnp.concatenate([hot_y[a], hot_y[a + 1]], axis=1)
        for values in (his, los):
            placed = jnp.concatenate(
                [
                    jnp.concatenate(
                        [jnp.where(on[i], values[p][i : i + 1, :], 0.0).astype(BF16) for i in (a, a + 1)], axis=1
                    )
                    for p in range(6)
                ],
                axis=0,
            )
            grid += mm(placed, wide, NT)

    left = jnp.concatenate(
        [
            jnp.concatenate([grid[2 * z * KX : (2 * z + 1) * KX], grid[(2 * z + 1) * KX : (2 * z + 2) * KX]], axis=1)
            for z in range(PLANES)
        ],
        axis=0,
    )
    inv_y = mm_right(left, wiy)
    planes = []
    for z in range(PLANES):
        rows = inv_y[z * KX : (z + 1) * KX]
        right = jnp.concatenate([rows[:, :V], rows[:, V:]], axis=0)
        grid_z = mm_left(wix, right)
        value = jnp.concatenate(
            [
                jnp.concatenate([field_pot[i, pl.ds(32 * x + z, 8, stride=4), :] for i in range(2)], axis=1)
                for x in range(U // 8)
            ],
            axis=0,
        )
        planes.append(jnp.concatenate([grid_z[:U] * value, grid_z[U:] * value], axis=1))
    fwd_y = mm_right(jnp.concatenate(planes, axis=0), wfy)
    right = jnp.concatenate(
        [
            jnp.concatenate([fwd_y[z * U : (z + 1) * U, :KY], fwd_y[z * U : (z + 1) * U, KY:]], axis=0)
            for z in range(PLANES)
        ],
        axis=1,
    )
    back = mm_left(wfx, right)
    stack = jnp.concatenate(
        [back[c * KX : (c + 1) * KX, z * KY : (z + 1) * KY] for z in range(PLANES) for c in range(2)], axis=0
    )
    both = jnp.concatenate(split(stack), axis=1)
    picked = [[] for _ in range(6)]
    for a in range(0, 8, 2):
        wide = jnp.concatenate([hot_y[a], hot_y[a + 1]], axis=1)
        spread = mm(both, jnp.concatenate([wide, wide], axis=0))
        for i in range(2):
            for p in range(6):
                block = spread[p * KX : (p + 1) * KX, 128 * i : 128 * (i + 1)]
                picked[p].append(jnp.sum(jnp.where(on[a + i], block, 0.0), axis=0, keepdims=True))
    picked = [jnp.concatenate(rows, axis=0) for rows in picked] + [jnp.zeros((8, 128), F32)] * 2
    for h in range(2):
        for b in range(4):
            rows = None
            for q in range(4):
                shift = 32 * ((q - b) % 4)
                turned = pltpu.roll(picked[4 * h + q], shift, 1) if shift else picked[4 * h + q]
                rows = turned if q == 0 else jnp.where(lane == q, turned, rows)
            for a in range(8):
                tiles[4 * a + b, h : h + 1, :] = rows[a : a + 1, :]
    ret[me] = tiles[0]

    for dz, dx in OFFSETS:
        pltpu.make_async_remote_copy(
            tiles.at[4 * dz + dx], ret.at[me], sb, rb, device_id={"fft": fft_at(8 - dz, 4 - dx)}, device_id_type=MESH
        ).start()

    total = jnp.sum(parts[1][3], axis=0, keepdims=True)
    total = total + pltpu.roll(total, 64, 1)
    total = total + pltpu.roll(total, 32, 1)
    c_re = jnp.sum(dfull * total[:, 0:16], axis=1, keepdims=True)
    c_im = jnp.sum(dfull * total[:, 16:32], axis=1, keepdims=True)
    for r in range(16):
        lanes = slice(128 * r, 128 * (r + 1))
        p_re, p_im = proj[0, :, lanes], proj[1, :, lanes]
        nonl[0, r : r + 1, :] = jnp.sum(c_re * p_re - c_im * p_im, axis=0, keepdims=True)
        nonl[1, r : r + 1, :] = jnp.sum(c_re * p_im + c_im * p_re, axis=0, keepdims=True)

    near[2].wait_recv()
    near[3].wait_recv()
    for c in far:
        c.wait_recv()
    swap = pltpu.make_async_remote_copy(
        pool.at[core], pool.at[core], sf, rf, device_id={"band": twin}, device_id_type=MESH
    )
    swap.start()

    sign = jnp.where(lax.broadcasted_iota(jnp.int32, (8, 128), 0) < 4, 1.0, -1.0)

    def correlate(at):
        def step(r, carry):
            u, w = carry
            block = pool[:, :, :, pl.ds(pl.multiple_of(128 * r, 128), 128)]
            u = u + block * vecs[at, pl.ds(r, 1), :]
            w = w + block * vecs[at + 1, pl.ds(r, 1), :]
            return u, w

        zero = jnp.zeros((2, 8, 8, 128), F32)
        u, w = lax.fori_loop(0, 16, step, (zero, zero))
        pieces = []
        for k in range(16):
            x = w[k % 2, k // 2]
            pieces.append(jnp.concatenate([x[4:8], x[0:4]], axis=0) + u[k % 2, k // 2] * sign)
        return mm(ones, jnp.concatenate(pieces, axis=0), NT, HIGHEST)[0:1, :]

    vecs[0] = m_re
    vecs[1] = m_im
    base_re = kin * m_re + nonl[0]
    base_im = kin * m_im + nonl[1]
    swap.wait_recv()
    s_row = correlate(0)

    every = pltpu.make_async_remote_copy(
        tiles.at[pl.ds(1, NF - 1)], ret.at[pl.ds(0, NF - 1)], sb, rb, device_id={"fft": fft_at(0, 1)}, device_id_type=MESH
    )
    every.wait_recv()
    came = jnp.concatenate([ret[d] for d in range(NF)], axis=0)
    came = jnp.concatenate([came] + [pltpu.roll(came, 128 - 32 * q, 1) for q in range(1, 4)], axis=0)
    loc = mm_left(tback, jnp.concatenate([came * cosp, came * sinp], axis=0)).T
    loc_re = jnp.concatenate([loc[0:16, :GZ], loc[16:32, :GZ]], axis=1)
    loc_im = jnp.concatenate([loc[0:16, GZ:], loc[16:32, GZ:]], axis=1)
    a_re = jnp.where(mask, base_re + loc_re, 0.0)
    a_im = jnp.where(mask, base_im + loc_im, 0.0)
    vecs[2] = a_re
    vecs[3] = a_im
    out[0] = a_re
    out[1] = a_im
    h_row = correlate(2)
    red[me] = jnp.concatenate([h_row, s_row], axis=0)
    for dz, dx in OFFSETS:
        pltpu.make_async_remote_copy(
            red.at[me], red.at[me], sr, rr, device_id={"fft": fft_at(dz, dx)}, device_id_type=MESH
        ).start()

    whole.wait_send()
    every.wait_send()
    for c in near:
        c.wait_send()
    for c in far:
        c.wait_send()
    swap.wait_send()
    last = pltpu.make_async_remote_copy(
        red.at[pl.ds(0, NF - 1)], red.at[pl.ds(0, NF - 1)], sr, rr, device_id={"fft": fft_at(0, 1)}, device_id_type=MESH
    )
    last.wait_recv()
    out_sums[...] = jnp.concatenate([jnp.sum(red[...], axis=0), jnp.zeros((6, 128), F32)], axis=0)
    last.wait_send()


def finish(applied, sums, out, out_h, out_s):
    out[...] = applied[...]
    li = lax.broadcasted_iota(jnp.int32, (128, 128), 0)
    lo = lax.broadcasted_iota(jnp.int32, (128, 128), 1)
    want = (lax.rem(lo, 64) // 4) * 8 + (lo // 64) * 4 + lax.rem(lo, 4)
    final = mm(sums[...], (li == want).astype(F32), NN, HIGHEST)
    out_h[0] = final[0:1, 0:64]
    out_h[1] = final[0:1, 64:128]
    out_s[0] = final[1:2, 0:64]
    out_s[1] = final[1:2, 64:128]


def shards(orbitals, stick_columns, stick_depths, potential, projectors, atom_projectors, couplings, slab_orbitals):
    args = (
        orbitals.reshape(2, 16, 128),
        stick_columns.reshape(1, STK),
        stick_depths,
        potential,
        projectors,
        atom_projectors,
        couplings,
        slab_orbitals,
    ) + tuple(jnp.asarray(t) for t in tables())
    vmem = pl.BlockSpec(memory_space=pltpu.VMEM)
    hbm = pl.BlockSpec(memory_space=pltpu.HBM)
    dma = pltpu.SemaphoreType.DMA
    applied, sums = pl.pallas_call(
        kernel,
        out_shape=(jax.ShapeDtypeStruct((2, 16, 128), F32), jax.ShapeDtypeStruct((8, 128), F32)),
        in_specs=[hbm] * len(args),
        out_specs=(vmem, vmem),
        scratch_shapes=[pltpu.VMEM(a.shape, a.dtype) for a in args]
        + [
            pltpu.VMEM((NF, 2, 128), F32),
            pltpu.VMEM((NF, 2, 128), F32),
            pltpu.VMEM((NF, 2, 128), F32),
            pltpu.VMEM((NF, 2, 128), F32),
            pltpu.VMEM((2, 8, 8, 2048), F32),
            pltpu.VMEM((NF, 2, 128), F32),
            pltpu.VMEM((2, 16, 128), F32),
            pltpu.VMEM((4, 16, 128), F32),
            pltpu.VMEM((2, 4 * U, 128), F32),
            dma((len(args),)),
        ]
        + [dma] * 4
        + [dma((4,))] * 4
        + [dma] * 4,
        compiler_params=pltpu.CompilerParams(
            collective_id=0, has_side_effects=True, vmem_limit_bytes=64 * 1024 * 1024
        ),
        name="davidson",
    )(*args)
    applied, proj_h, proj_s = pl.pallas_call(
        finish,
        out_shape=(
            jax.ShapeDtypeStruct((2, 16, 128), F32),
            jax.ShapeDtypeStruct((2, 1, 64), F32),
            jax.ShapeDtypeStruct((2, 1, 64), F32),
        ),
        in_specs=[vmem, vmem],
        out_specs=(vmem, vmem, vmem),
        name="finish",
    )(applied, sums)
    return applied.reshape(2, 1, 2048), proj_h, proj_s


def solution(mesh):
    in_specs = (
        P(None, "band", "fft"),
        P("fft"),
        P("fft", None),
        P("fft", None),
        P(None, None, "fft"),
        P(),
        P(),
        P(None, "band", "fft"),
    )
    out_specs = (P(None, "band", "fft"), P(None, "band", None), P(None, "band", None))
    return jax.shard_map(shards, mesh=mesh, in_specs=in_specs, out_specs=out_specs, check_vma=False)
```

time: 48.6 us -> 40.5 us (0.83)
  the two profiles are of different devices: /device:TPU:1 before, /device:TPU:16 now
where the time goes in v2:
time: 40.5 us; the launch traced here: 40.2 us
  Pallas kernels  39.5 us (98%)
  between operations  0.64 us (2%)
    pallas_call x1, Pallas kernels, shards(): pl.pallas_call(kernel, out_shape=(jax.ShapeDtypeStruct((2, 16, 128), F32)...  38 us
    pallas_call x1, Pallas kernels, shards(): pl.pallas_call(finish, out_shape=(jax.ShapeDtypeStruct((2, 16, 128), F32)...  1.53 us

profile of v2, /device:TPU:16, one launch (start us, length us, event | category | flops | bytes accessed | tf_op | source)
XLA Modules:
  0.0 40.2 jit_solution(852876496375650714)
XLA Ops:
  0.6 38.0 %davidson.1 = (f32[2,16,128]{2,1,0:T(8,128)}, f32[8,128]{1,0:T(8,128)}) custom-call(f32[2,16,128]{2,1,0:T(8,128)} %bitcast.3, s32[1,32]{1,0:T(1,128)} %bitcast.4, s32[32,64]{1,0:T(8,128)} %deps_h.1, f32[3,32400]{1,0:T(4,128)} %pot_h.1, f32[2,16,2048]{2,1,0:T(8,128)} %proj_h.1, s32[2,8]{1,0:T(2,128)} %atoms_h.1, f32[2,8,8]{2,1,0:T(8,128)} %coup_h.1, ...), custom_call_target="tpu_custom_call" | custom-call | tf_op jit(solution)/shard_map/davidson/pallas_call | solution.py:503
  38.6 1.5 %finish.1 = (f32[2,16,128]{2,1,0:T(8,128)}, f32[2,1,64]{2,1,0:T(1,128)}, f32[2,1,64]{2,1,0:T(1,128)}) custom-call(f32[2,16,128]{2,1,0:T(8,128)} %get-tuple-element.8.applied, f32[8,128]{1,0:T(8,128)} %get-tuple-element.9.sums), custom_call_target="tpu_custom_call" | custom-call | tf_op jit(solution)/shard_map/finish/pallas_call | solution.py:529

commit v3 on v2

--- a/solution.py
+++ b/solution.py
@@ -18,9 +18,9 @@
 NXY = NX * NY
 NF = 32
 STK = 32
-KX = 96
-KY = 128
-U = 192
+KA = 48
+KB = 64
+U = 96
 V = 256
 PLANES = 3
 
@@ -88,23 +88,21 @@
             ph = tau * (depth * z % NZ) / NZ
             turn[0, q, d, h, : NZ + 1] = np.cos(ph)
             turn[1, q, d, h, : NZ + 1] = np.sin(ph)
-    n = 2 * RADIUS + 1
-    k = np.arange(n) - RADIUS
-    g = np.arange(NX)
+    n = RADIUS + 1
+    k = np.arange(n)
+    ang = tau * ((k[:, None] * np.arange(NY)[None, :]) % NY) / NY
+    wiy = np.zeros((2, KB, V))
+    wiy[0, :n, :NY], wiy[1, :n, :NY] = np.cos(ang) / NY, np.sin(ang) / NY
+    wfy = np.zeros((V, 2, KB))
+    wfy[:NY, 0, :n], wfy[:NY, 1, :n] = np.cos(ang).T, np.sin(ang).T
+    g = np.arange(NX // 2 + 1)
     ang = tau * ((k[:, None] * g[None, :]) % NX) / NX
     c, s = np.cos(ang), np.sin(ang)
-    wiy = np.zeros((2, KY, 2, V))
-    wiy[0, :n, 0, :NY], wiy[0, :n, 1, :NY] = c / NY, s / NY
-    wiy[1, :n, 0, :NY], wiy[1, :n, 1, :NY] = -s / NY, c / NY
-    wix = np.zeros((2, U, 2, KX))
-    wix[0, :NX, 0, :n], wix[0, :NX, 1, :n] = c.T / NX, -s.T / NX
-    wix[1, :NX, 0, :n], wix[1, :NX, 1, :n] = s.T / NX, c.T / NX
-    wfy = np.zeros((2, V, 2, KY))
-    wfy[0, :NY, 0, :n], wfy[0, :NY, 1, :n] = c.T, -s.T
-    wfy[1, :NY, 0, :n], wfy[1, :NY, 1, :n] = s.T, c.T
-    wfx = np.zeros((2, KX, 2, U))
-    wfx[0, :n, 0, :NX], wfx[0, :n, 1, :NX] = c, s
-    wfx[1, :n, 0, :NX], wfx[1, :n, 1, :NX] = -s, c
+    wix = np.zeros((2, U, KA))
+    wix[0, : len(g), :n], wix[1, : len(g), :n] = c.T / NX, s.T / NX
+    wfx = np.zeros((2, KA, 2, U))
+    wfx[0, :n, 0, : len(g)], wfx[0, :n, 1, : len(g)] = c, c
+    wfx[1, :n, 0, : len(g)], wfx[1, :n, 1, : len(g)] = s, -s
     back = np.transpose(tb.reshape(2, GZ, 2, 256), (2, 1, 0, 3)).reshape(2 * GZ, 512)
     tz = np.concatenate([t1.reshape(256, 128), t2.reshape(256, 128)], axis=0) / NZ
 
@@ -114,13 +112,17 @@
         lo = (x - hi.astype(np.float32)).astype(ml_dtypes.bfloat16)
         return np.stack([hi, lo])
 
+    yh, yl = parts(wiy.reshape(2 * KB, V))
+    xh, xl = parts(wix)
+    fh, fl = parts(wfy.reshape(V, 2 * KB))
+    gh, gl = parts(wfx.reshape(2 * KA, 2 * U))
     return (
         parts(tz),
         parts(turn.reshape(512, 128)),
-        parts(wiy.reshape(2 * KY, 2 * V)),
-        parts(wix.reshape(2 * U, 2 * KX)),
-        parts(wfy.reshape(2 * V, 2 * KY)),
-        parts(wfx.reshape(2 * KX, 2 * U)),
+        np.concatenate([yh, yh, yl], axis=0),
+        np.concatenate([xh, xh, xl], axis=2),
+        np.concatenate([fh, fl], axis=1),
+        np.concatenate([gh, gl], axis=0),
         parts(back),
     )
 
@@ -130,7 +132,7 @@
     out, out_sums,
     orb, cols, deps, pot, proj, atoms, coup, slab, tz, turn, wiy, wix, wfy, wfx, tback,
     mine, got, tiles, ret, pool, red, nonl, vecs, field_pot,
-    loads, sa, ra, sb, rb, near_s, near_r, far_s, far_r, sf, rf, sr, rr,
+    loads, keep, sa, ra, sb, rb, near_s, near_r, far_s, far_r, sf, rf, sr, rr,
 ):
     me = lax.axis_index("fft")
     band = lax.axis_index("band")
@@ -190,13 +192,15 @@
     qx = jnp.floor((colf + 0.5) * (1.0 / NY))
     qy = colf - NY * qx
     live = cols[...] < NXY
-    kx = jnp.where(live, jnp.where(qx < 90.0, qx, qx - NX) + (RADIUS + 1), 0.0)
-    ky = jnp.where(live, jnp.where(qy < 90.0, qy, qy - NY) + (RADIUS + 1), 0.0)
+    far_x, far_y = qx >= 90.0, qy >= 90.0
+    kx = jnp.where(live, jnp.where(far_x, NX - qx, qx), 63.0)
+    ky = jnp.where(live, jnp.where(far_y, NY - qy, qy), 0.0)
+    col = ky + jnp.where(far_x, 2.0 * KB, 0.0) + jnp.where(far_y, 1.0 * KB, 0.0)
     si = lax.broadcasted_iota(jnp.int32, (STK, 128), 0)
     so = lax.rem(lax.broadcasted_iota(jnp.int32, (STK, 128), 1), 32)
     perm = (si == 2 * lax.rem(so, 16) + so // 16).astype(F32)
-    kxy = mm(jnp.concatenate([kx, ky, jnp.zeros((6, STK), F32)], axis=0), perm)
-    code = kxy[0:1, :] * 128.0 + kxy[1:2, :]
+    kxy = mm(jnp.concatenate([kx, col, jnp.zeros((6, STK), F32)], axis=0), perm)
+    code = kxy[0:1, :] * 256.0 + kxy[1:2, :]
 
     copies[5].wait()
     acc_re = jnp.zeros((16, 128), F32)
@@ -247,7 +251,20 @@
         )
 
     own = pool.at[core, row]
-    near = [to_band(own, own, near_s.at[i], near_r.at[i], dy) for i, dy in enumerate((2, 6, 1, 7))]
+    first_half, second_half = pl.ds(0, 1024), pl.ds(1024, 1024)
+    near = [
+        to_band(src, src, near_s.at[i], near_r.at[i], dy)
+        for i, (src, dy) in enumerate(
+            (
+                (own.at[:, first_half], 2),
+                (own.at[:, second_half], 6),
+                (own.at[:, second_half], 2),
+                (own.at[:, first_half], 6),
+                (own, 1),
+                (own, 7),
+            )
+        )
+    ]
     for c in near:
         c.start()
 
@@ -256,8 +273,8 @@
     s_i = lax.broadcasted_iota(jnp.int32, (STK, 128), 0)
     l_i = lax.broadcasted_iota(jnp.int32, (STK, 128), 1)
     half = (lax.rem(s_i, 2) == l_i // GZ).astype(F32)
-    kx16 = mm(jnp.where(sr_i == rr_i, jnp.broadcast_to(kx, (16, STK)), 0.0), half) - (RADIUS + 1)
-    ky16 = mm(jnp.where(sr_i == rr_i, jnp.broadcast_to(ky, (16, STK)), 0.0), half) - (RADIUS + 1)
+    kx16 = mm(jnp.where(sr_i == rr_i, jnp.broadcast_to(kx, (16, STK)), 0.0), half)
+    ky16 = mm(jnp.where(sr_i == rr_i, jnp.broadcast_to(ky, (16, STK)), 0.0), half)
     fz = jnp.where(dep16 < NZ // 2, dep16, dep16 - NZ).astype(F32)
     kin = (0.5 / (RADIUS * RADIUS)) * (kx16 * kx16 + ky16 * ky16 + fz * fz)
 
@@ -272,29 +289,40 @@
 
     field_pot[...] = jnp.zeros_like(field_pot)
     for x in range(NX):
-        field_pot[0, 4 * x : 4 * x + PLANES, :] = pot[:, NY * x : NY * x + 128]
-        field_pot[1, 4 * x : 4 * x + PLANES, 0 : NY - 128] = pot[:, NY * x + 128 : NY * x + NY]
+        r = 4 * (x if x <= NX // 2 else U + NX - x)
+        field_pot[0, r : r + PLANES, :] = pot[:, NY * x : NY * x + 128]
+        field_pot[1, r : r + PLANES, 0 : NY - 128] = pot[:, NY * x + 128 : NY * x + NY]
 
     ahead = pool.at[core, lax.rem(row + 6, 8)]
     behind = pool.at[core, lax.rem(row + 2, 8)]
-    first_half, second_half = pl.ds(0, 1024), pl.ds(1024, 1024)
-    far = (
-        to_band(ahead, ahead, far_s.at[0], far_r.at[0], 1),
-        to_band(ahead.at[:, first_half], ahead.at[:, first_half], far_s.at[1], far_r.at[1], 2),
-        to_band(behind, behind, far_s.at[2], far_r.at[2], 7),
-        to_band(behind.at[:, second_half], behind.at[:, second_half], far_s.at[3], far_r.at[3], 6),
-    )
-
-    whole = pltpu.make_async_remote_copy(
-        got.at[pl.ds(1, NF - 1)], got.at[pl.ds(1, NF - 1)], sa, ra, device_id={"fft": fft_at(0, 1)}, device_id_type=MESH
-    )
-    whole.wait_recv()
+    far = [
+        to_band(src, src, far_s.at[i], far_r.at[i], dy)
+        for i, (src, dy) in enumerate(
+            (
+                (ahead.at[:, first_half], 2),
+                (ahead.at[:, first_half], 1),
+                (behind.at[:, second_half], 6),
+                (behind.at[:, second_half], 7),
+                (ahead.at[:, second_half], 1),
+                (behind.at[:, first_half], 7),
+            )
+        )
+    ]
     near[0].wait_recv()
     far[0].start()
     far[1].start()
     near[1].wait_recv()
     far[2].start()
     far[3].start()
+    near[2].wait_recv()
+    far[4].start()
+    near[3].wait_recv()
+    far[5].start()
+
+    whole = pltpu.make_async_remote_copy(
+        got.at[pl.ds(1, NF - 1)], got.at[pl.ds(1, NF - 1)], sa, ra, device_id={"fft": fft_at(0, 1)}, device_id_type=MESH
+    )
+    whole.wait_recv()
 
     lane = lax.broadcasted_iota(jnp.int32, (8, 128), 1) // 32
     parts = [[None] * 4 for _ in range(2)]
@@ -307,20 +335,18 @@
                 parts[h][q] = turned if b == 0 else jnp.where(lane == b, turned, parts[h][q])
     fields = [parts[p // 4][p % 4] for p in range(6)]
     code = parts[1][2]
-    kx_at = jnp.floor(code * (1.0 / 128.0))
-    ky_at = code - 128.0 * kx_at
-    kx_at -= 1.0
-    ky_at -= 1.0
-
-    ix = lax.broadcasted_iota(jnp.int32, (KX, 128), 0).astype(F32)
-    iy = lax.broadcasted_iota(jnp.int32, (KY, 128), 0).astype(F32)
+    kx_at = jnp.floor(code * (1.0 / 256.0))
+    col_at = code - 256.0 * kx_at
+
+    ix = lax.broadcasted_iota(jnp.int32, (KA, 128), 0).astype(F32)
+    iy = lax.broadcasted_iota(jnp.int32, (4 * KB, 128), 0).astype(F32)
     his = [f.astype(BF16).astype(F32) for f in fields]
     los = [f - h for f, h in zip(fields, his)]
     on = [ix == kx_at[a : a + 1, :] for a in range(8)]
-    hot_y = [(iy == ky_at[a : a + 1, :]).astype(F32).astype(BF16) for a in range(8)]
-    grid = jnp.zeros((6 * KX, KY), F32)
+    hot_y = [(iy == col_at[a : a + 1, :]).astype(F32).astype(BF16) for a in range(8)]
+    wide = [jnp.concatenate(hot_y[a : a + 2], axis=1) for a in range(0, 8, 2)]
+    grid = jnp.zeros((6 * KA, 4 * KB), F32)
     for a in range(0, 8, 2):
-        wide = jnp.concatenate([hot_y[a], hot_y[a + 1]], axis=1)
         for values in (his, los):
             placed = jnp.concatenate(
                 [
@@ -331,49 +357,71 @@
                 ],
                 axis=0,
             )
-            grid += mm(placed, wide, NT)
-
-    left = jnp.concatenate(
-        [
-            jnp.concatenate([grid[2 * z * KX : (2 * z + 1) * KX], grid[(2 * z + 1) * KX : (2 * z + 2) * KX]], axis=1)
-            for z in range(PLANES)
-        ],
-        axis=0,
-    )
-    inv_y = mm_right(left, wiy)
+            grid += mm(placed, wide[a // 2], NT)
+
+    low = lax.broadcasted_iota(jnp.int32, (KA, 2 * KB), 1) < KB
+    rows = []
+    for z in range(PLANES):
+        real, imag = grid[2 * z * KA : (2 * z + 1) * KA], grid[(2 * z + 1) * KA : (2 * z + 2) * KA]
+        pair = []
+        for s in range(2):
+            re, im = real[:, 128 * s : 128 * (s + 1)], imag[:, 128 * s : 128 * (s + 1)]
+            re_t, im_t = pltpu.roll(re, KB, 1), pltpu.roll(im, KB, 1)
+            pair.append((jnp.where(low, re + re_t, im - im_t), jnp.where(low, im + im_t, re_t - re)))
+        rows += [pair[0][0], pair[1][0], pair[0][1], pair[1][1]]
+    hi, lo = split(jnp.concatenate(rows, axis=0))
+    inv_y = mm(jnp.concatenate([hi, lo], axis=1), wiy[0:256, :]) + mm(hi, wiy[256:384, :])
+
     planes = []
     for z in range(PLANES):
-        rows = inv_y[z * KX : (z + 1) * KX]
-        right = jnp.concatenate([rows[:, :V], rows[:, V:]], axis=0)
-        grid_z = mm_left(wix, right)
-        value = jnp.concatenate(
-            [
-                jnp.concatenate([field_pot[i, pl.ds(32 * x + z, 8, stride=4), :] for i in range(2)], axis=1)
-                for x in range(U // 8)
-            ],
-            axis=0,
-        )
-        planes.append(jnp.concatenate([grid_z[:U] * value, grid_z[U:] * value], axis=1))
-    fwd_y = mm_right(jnp.concatenate(planes, axis=0), wfy)
-    right = jnp.concatenate(
-        [
-            jnp.concatenate([fwd_y[z * U : (z + 1) * U, :KY], fwd_y[z * U : (z + 1) * U, KY:]], axis=0)
-            for z in range(PLANES)
-        ],
-        axis=1,
-    )
-    back = mm_left(wfx, right)
-    stack = jnp.concatenate(
-        [back[c * KX : (c + 1) * KX, z * KY : (z + 1) * KY] for z in range(PLANES) for c in range(2)], axis=0
-    )
-    both = jnp.concatenate(split(stack), axis=1)
+        part4 = [inv_y[(4 * z + i) * KA : (4 * z + i + 1) * KA] for i in range(4)]
+        even = jnp.concatenate([part4[0] + part4[1], part4[2] + part4[3]], axis=1)
+        odd = jnp.concatenate([part4[2] - part4[3], part4[0] - part4[1]], axis=1)
+        made = []
+        for t, values in enumerate((even, odd)):
+            hi, lo = split(values)
+            made.append(mm(wix[t], jnp.concatenate([hi, lo, hi], axis=0)))
+        value = [
+            jnp.concatenate(
+                [
+                    jnp.concatenate([field_pot[i, pl.ds(32 * x + z, 8, stride=4), :] for i in range(2)], axis=1)
+                    for x in range(f * U // 8, (f + 1) * U // 8)
+                ],
+                axis=0,
+            )
+            for f in range(2)
+        ]
+        e_re, e_im, o_im, o_re = made[0][:, :V], made[0][:, V:], made[1][:, :V], made[1][:, V:]
+        planes += [
+            (e_re - o_im) * value[0],
+            (e_re + o_im) * value[1],
+            (e_im + o_re) * value[0],
+            (e_im - o_re) * value[1],
+        ]
+    hi, lo = split(jnp.concatenate(planes, axis=0))
+    fwd_y = mm(hi, wfy[...]) + mm(lo, wfy[...])
+    fwd_y = fwd_y[:, :128] + fwd_y[:, 128:]
+    stack = []
+    for z in range(PLANES):
+        right = jnp.concatenate([fwd_y[4 * z * U : (4 * z + 2) * U], fwd_y[(4 * z + 2) * U : (4 * z + 4) * U]], axis=1)
+        hi, lo = split(right)
+        all_hi = mm(wfx[...], hi)
+        sums = all_hi[: 2 * KA] + (all_hi[2 * KA :] + mm(wfx[0 : 2 * KA, :], lo))
+        c_re, c_im, s_re, s_im = sums[:KA, :128], sums[:KA, 128:], sums[KA:, :128], sums[KA:, 128:]
+        real, imag = [], []
+        for p, q in ((c_re + s_im, c_im - s_re), (c_re - s_im, c_im + s_re)):
+            m, n = jnp.where(low, p, q), jnp.where(low, q, -p)
+            m_t, n_t = pltpu.roll(m, KB, 1), pltpu.roll(n, KB, 1)
+            real.append(jnp.where(low, m + m_t, m_t - m))
+            imag.append(jnp.where(low, n + n_t, n_t - n))
+        stack += [jnp.concatenate(real, axis=1), jnp.concatenate(imag, axis=1)]
+    hi, lo = split(jnp.concatenate(stack, axis=0))
     picked = [[] for _ in range(6)]
     for a in range(0, 8, 2):
-        wide = jnp.concatenate([hot_y[a], hot_y[a + 1]], axis=1)
-        spread = mm(both, jnp.concatenate([wide, wide], axis=0))
+        spread = mm(hi, wide[a // 2]) + mm(lo, wide[a // 2])
         for i in range(2):
             for p in range(6):
-                block = spread[p * KX : (p + 1) * KX, 128 * i : 128 * (i + 1)]
+                block = spread[p * KA : (p + 1) * KA, 128 * i : 128 * (i + 1)]
                 picked[p].append(jnp.sum(jnp.where(on[a + i], block, 0.0), axis=0, keepdims=True))
     picked = [jnp.concatenate(rows, axis=0) for rows in picked] + [jnp.zeros((8, 128), F32)] * 2
     for h in range(2):
@@ -403,16 +451,21 @@
         nonl[0, r : r + 1, :] = jnp.sum(c_re * p_re - c_im * p_im, axis=0, keepdims=True)
         nonl[1, r : r + 1, :] = jnp.sum(c_re * p_im + c_im * p_re, axis=0, keepdims=True)
 
-    near[2].wait_recv()
-    near[3].wait_recv()
+    def pass_on(k):
+        block = pool.at[core, lax.rem(row + k, 8)]
+        pltpu.make_async_remote_copy(block, block, sf, rf, device_id={"band": twin}, device_id_type=MESH).start()
+
+    near[4].wait_recv()
+    near[5].wait_recv()
+    for k in (0, 1, 2, 6, 7):
+        pass_on(k)
     for c in far:
         c.wait_recv()
+    for k in (3, 4, 5):
+        pass_on(k)
     swap = pltpu.make_async_remote_copy(
         pool.at[core], pool.at[core], sf, rf, device_id={"band": twin}, device_id_type=MESH
     )
-    swap.start()
-
-    sign = jnp.where(lax.broadcasted_iota(jnp.int32, (8, 128), 0) < 4, 1.0, -1.0)
 
     def correlate(at):
         def step(r, carry):
@@ -424,11 +477,9 @@
 
         zero = jnp.zeros((2, 8, 8, 128), F32)
         u, w = lax.fori_loop(0, 16, step, (zero, zero))
-        pieces = []
-        for k in range(16):
-            x = w[k % 2, k // 2]
-            pieces.append(jnp.concatenate([x[4:8], x[0:4]], axis=0) + u[k % 2, k // 2] * sign)
-        return mm(ones, jnp.concatenate(pieces, axis=0), NT, HIGHEST)[0:1, :]
+        real = [u[k % 2, k // 2][0:4] + w[k % 2, k // 2][4:8] for k in range(16)]
+        imag = [w[k % 2, k // 2][0:4] - u[k % 2, k // 2][4:8] for k in range(16)]
+        return mm(ones, jnp.concatenate(real + imag, axis=0), NT, HIGHEST)[0:1, :]
 
     vecs[0] = m_re
     vecs[1] = m_im
@@ -450,8 +501,8 @@
     a_im = jnp.where(mask, base_im + loc_im, 0.0)
     vecs[2] = a_re
     vecs[3] = a_im
-    out[0] = a_re
-    out[1] = a_im
+    store = pltpu.make_async_copy(vecs.at[pl.ds(2, 2)], out, keep)
+    store.start()
     h_row = correlate(2)
     red[me] = jnp.concatenate([h_row, s_row], axis=0)
     for dz, dx in OFFSETS:
@@ -470,20 +521,16 @@
         red.at[pl.ds(0, NF - 1)], red.at[pl.ds(0, NF - 1)], sr, rr, device_id={"fft": fft_at(0, 1)}, device_id_type=MESH
     )
     last.wait_recv()
-    out_sums[...] = jnp.concatenate([jnp.sum(red[...], axis=0), jnp.zeros((6, 128), F32)], axis=0)
+    out_sums[...] = jnp.sum(red[...], axis=0)
     last.wait_send()
+    store.wait()
 
 
 def finish(applied, sums, out, out_h, out_s):
     out[...] = applied[...]
-    li = lax.broadcasted_iota(jnp.int32, (128, 128), 0)
-    lo = lax.broadcasted_iota(jnp.int32, (128, 128), 1)
-    want = (lax.rem(lo, 64) // 4) * 8 + (lo // 64) * 4 + lax.rem(lo, 4)
-    final = mm(sums[...], (li == want).astype(F32), NN, HIGHEST)
-    out_h[0] = final[0:1, 0:64]
-    out_h[1] = final[0:1, 64:128]
-    out_s[0] = final[1:2, 0:64]
-    out_s[1] = final[1:2, 64:128]
+    for c in range(2):
+        out_h[c] = sums[0:1, 64 * c : 64 * (c + 1)]
+        out_s[c] = sums[1:2, 64 * c : 64 * (c + 1)]
 
 
 def shards(orbitals, stick_columns, stick_depths, potential, projectors, atom_projectors, couplings, slab_orbitals):
@@ -502,9 +549,9 @@
     dma = pltpu.SemaphoreType.DMA
     applied, sums = pl.pallas_call(
         kernel,
-        out_shape=(jax.ShapeDtypeStruct((2, 16, 128), F32), jax.ShapeDtypeStruct((8, 128), F32)),
+        out_shape=(jax.ShapeDtypeStruct((2, 16, 128), F32), jax.ShapeDtypeStruct((2, 128), F32)),
         in_specs=[hbm] * len(args),
-        out_specs=(vmem, vmem),
+        out_specs=(hbm, vmem),
         scratch_shapes=[pltpu.VMEM(a.shape, a.dtype) for a in args]
         + [
             pltpu.VMEM((NF, 2, 128), F32),
@@ -515,11 +562,11 @@
             pltpu.VMEM((NF, 2, 128), F32),
             pltpu.VMEM((2, 16, 128), F32),
             pltpu.VMEM((4, 16, 128), F32),
-            pltpu.VMEM((2, 4 * U, 128), F32),
+            pltpu.VMEM((2, 8 * U, 128), F32),
             dma((len(args),)),
         ]
-        + [dma] * 4
-        + [dma((4,))] * 4
+        + [dma] * 5
+        + [dma((6,))] * 4
         + [dma] * 4,
         compiler_params=pltpu.CompilerParams(
             collective_id=0, has_side_effects=True, vmem_limit_bytes=64 * 1024 * 1024
@@ -535,6 +582,7 @@
         ),
         in_specs=[vmem, vmem],
         out_specs=(vmem, vmem, vmem),
+        compiler_params=pltpu.CompilerParams(vmem_limit_bytes=64 * 1024 * 1024),
         name="finish",
     )(applied, sums)
     return applied.reshape(2, 1, 2048), proj_h, proj_s

time: 40.5 us -> 38.7 us (0.956)
  the two profiles are of different devices: /device:TPU:16 before, /device:TPU:24 now
where the time goes in v3:
time: 38.7 us; the launch traced here: 38.4 us
  Pallas kernels  37.7 us (97%)
  between operations  0.64 us (2%)
    pallas_call x1, Pallas kernels, shards(): pl.pallas_call(kernel, out_shape=(jax.ShapeDtypeStruct((2, 16, 128), F32)...  36.4 us
    pallas_call x1, Pallas kernels, shards(): pl.pallas_call(finish, out_shape=(jax.ShapeDtypeStruct((2, 16, 128), F32)...  1.36 us

profile of v3, /device:TPU:24, one launch (start us, length us, event | category | flops | bytes accessed | tf_op | source)
XLA Modules:
  0.0 38.4 jit_solution(3317211423253559327)
XLA Ops:
  0.6 36.4 %davidson.1 = (f32[2,16,128]{2,1,0:T(8,128)}, f32[2,128]{1,0:T(2,128)}) custom-call(f32[2,16,128]{2,1,0:T(8,128)} %bitcast.3, s32[1,32]{1,0:T(1,128)} %bitcast.4, s32[32,64]{1,0:T(8,128)} %deps_h.1, f32[3,32400]{1,0:T(4,128)} %pot_h.1, f32[2,16,2048]{2,1,0:T(8,128)} %proj_h.1, s32[2,8]{1,0:T(2,128)} %atoms_h.1, f32[2,8,8]{2,1,0:T(8,128)} %coup_h.1, ...), custom_call_target="tpu_custom_call" | custom-call | tf_op jit(solution)/shard_map/davidson/pallas_call | solution.py:550
  37.0 1.4 %finish.1 = (f32[2,16,128]{2,1,0:T(8,128)}, f32[2,1,64]{2,1,0:T(1,128)}, f32[2,1,64]{2,1,0:T(1,128)}) custom-call(f32[2,16,128]{2,1,0:T(8,128)} %get-tuple-element.8.applied, f32[2,128]{1,0:T(2,128)} %get-tuple-element.9.sums), custom_call_target="tpu_custom_call" | custom-call | tf_op jit(solution)/shard_map/finish/pallas_call | solution.py:576

commit v4 on v3

--- a/solution.py
+++ b/solution.py
@@ -132,7 +132,7 @@
     out, out_sums,
     orb, cols, deps, pot, proj, atoms, coup, slab, tz, turn, wiy, wix, wfy, wfx, tback,
     mine, got, tiles, ret, pool, red, nonl, vecs, field_pot,
-    loads, keep, sa, ra, sb, rb, near_s, near_r, far_s, far_r, sf, rf, sr, rr,
+    loads, sa, ra, sb, rb, near_s, near_r, far_s, far_r, sf, rf, sr, rr,
 ):
     me = lax.axis_index("fft")
     band = lax.axis_index("band")
@@ -308,17 +308,6 @@
             )
         )
     ]
-    near[0].wait_recv()
-    far[0].start()
-    far[1].start()
-    near[1].wait_recv()
-    far[2].start()
-    far[3].start()
-    near[2].wait_recv()
-    far[4].start()
-    near[3].wait_recv()
-    far[5].start()
-
     whole = pltpu.make_async_remote_copy(
         got.at[pl.ds(1, NF - 1)], got.at[pl.ds(1, NF - 1)], sa, ra, device_id={"fft": fft_at(0, 1)}, device_id_type=MESH
     )
@@ -399,6 +388,17 @@
             (e_im - o_re) * value[1],
         ]
     hi, lo = split(jnp.concatenate(planes, axis=0))
+    near[0].wait_recv()
+    far[0].start()
+    far[1].start()
+    near[1].wait_recv()
+    far[2].start()
+    far[3].start()
+    near[2].wait_recv()
+    far[4].start()
+    near[3].wait_recv()
+    far[5].start()
+
     fwd_y = mm(hi, wfy[...]) + mm(lo, wfy[...])
     fwd_y = fwd_y[:, :128] + fwd_y[:, 128:]
     stack = []
@@ -485,8 +485,6 @@
     vecs[1] = m_im
     base_re = kin * m_re + nonl[0]
     base_im = kin * m_im + nonl[1]
-    swap.wait_recv()
-    s_row = correlate(0)
 
     every = pltpu.make_async_remote_copy(
         tiles.at[pl.ds(1, NF - 1)], ret.at[pl.ds(0, NF - 1)], sb, rb, device_id={"fft": fft_at(0, 1)}, device_id_type=MESH
@@ -501,8 +499,10 @@
     a_im = jnp.where(mask, base_im + loc_im, 0.0)
     vecs[2] = a_re
     vecs[3] = a_im
-    store = pltpu.make_async_copy(vecs.at[pl.ds(2, 2)], out, keep)
-    store.start()
+    out[0] = a_re
+    out[1] = a_im
+    swap.wait_recv()
+    s_row = correlate(0)
     h_row = correlate(2)
     red[me] = jnp.concatenate([h_row, s_row], axis=0)
     for dz, dx in OFFSETS:
@@ -523,7 +523,6 @@
     last.wait_recv()
     out_sums[...] = jnp.sum(red[...], axis=0)
     last.wait_send()
-    store.wait()
 
 
 def finish(applied, sums, out, out_h, out_s):
@@ -549,9 +548,9 @@
     dma = pltpu.SemaphoreType.DMA
     applied, sums = pl.pallas_call(
         kernel,
-        out_shape=(jax.ShapeDtypeStruct((2, 16, 128), F32), jax.ShapeDtypeStruct((2, 128), F32)),
+        out_shape=(pltpu.VMEM((2, 16, 128), F32), pltpu.VMEM((2, 128), F32)),
         in_specs=[hbm] * len(args),
-        out_specs=(hbm, vmem),
+        out_specs=(vmem, vmem),
         scratch_shapes=[pltpu.VMEM(a.shape, a.dtype) for a in args]
         + [
             pltpu.VMEM((NF, 2, 128), F32),
@@ -565,11 +564,11 @@
             pltpu.VMEM((2, 8 * U, 128), F32),
             dma((len(args),)),
         ]
-        + [dma] * 5
+        + [dma] * 4
         + [dma((6,))] * 4
         + [dma] * 4,
         compiler_params=pltpu.CompilerParams(
-            collective_id=0, has_side_effects=True, vmem_limit_bytes=64 * 1024 * 1024
+            collective_id=0, has_side_effects=True, vmem_limit_bytes=65024 * 1024
         ),
         name="davidson",
     )(*args)
@@ -582,7 +581,7 @@
         ),
         in_specs=[vmem, vmem],
         out_specs=(vmem, vmem, vmem),
-        compiler_params=pltpu.CompilerParams(vmem_limit_bytes=64 * 1024 * 1024),
+        compiler_params=pltpu.CompilerParams(vmem_limit_bytes=1024 * 1024),
         name="finish",
     )(applied, sums)
     return applied.reshape(2, 1, 2048), proj_h, proj_s

time: 38.7 us -> 36.9 us (0.953)
  the two profiles are of different devices: /device:TPU:24 before, /device:TPU:1 now
where the time goes in v4:
time: 36.9 us; the launch traced here: 36.7 us
  Pallas kernels  36.1 us (98%)
  between operations  0.64 us (2%)
    pallas_call x1, Pallas kernels, shards(): pl.pallas_call(kernel, out_shape=(pltpu.VMEM((2, 16, 128), F32), pltpu.VM...  35.5 us

profile of v4, /device:TPU:1, one launch (start us, length us, event | category | flops | bytes accessed | tf_op | source)
XLA Modules:
  0.0 36.7 jit_solution(1779377230861129978)
XLA Ops:
  0.6 35.5 %davidson.1 = (f32[2,16,128]{2,1,0:T(8,128)S(1)}, f32[2,128]{1,0:T(2,128)S(1)}) custom-call(f32[2,16,128]{2,1,0:T(8,128)} %bitcast.3, s32[1,32]{1,0:T(1,128)} %bitcast.4, s32[32,64]{1,0:T(8,128)} %deps_h.1, f32[3,32400]{1,0:T(4,128)} %pot_h.1, f32[2,16,2048]{2,1,0:T(8,128)} %proj_h.1, s32[2,8]{1,0:T(2,128)} %atoms_h.1, f32[2,8,8]{2,1,0:T(8,128)} %coup_h.1, ...), custom_call_target="tpu_custom_call" | custom-call | tf_op jit(solution)/shard_map/davidson/pallas_call | solution.py:549
  36.1 0.6 %finish.1 = (f32[2,16,128]{2,1,0:T(8,128)}, f32[2,1,64]{2,1,0:T(1,128)}, f32[2,1,64]{2,1,0:T(1,128)}) custom-call(f32[2,16,128]{2,1,0:T(8,128)S(1)} %get-tuple-element.8.applied, f32[2,128]{1,0:T(2,128)S(1)} %get-tuple-element.9.sums), custom_call_target="tpu_custom_call" | custom-call | tf_op jit(solution)/shard_map/finish/pallas_call | solution.py:575

commit v5 on v4

--- a/solution.py
+++ b/solution.py
@@ -103,7 +103,7 @@
     wfx = np.zeros((2, KA, 2, U))
     wfx[0, :n, 0, : len(g)], wfx[0, :n, 1, : len(g)] = c, c
     wfx[1, :n, 0, : len(g)], wfx[1, :n, 1, : len(g)] = s, -s
-    back = np.transpose(tb.reshape(2, GZ, 2, 256), (2, 1, 0, 3)).reshape(2 * GZ, 512)
+    back = np.transpose(tb.reshape(2, GZ, 2, 256), (0, 3, 2, 1)).reshape(512, 2 * GZ)
     tz = np.concatenate([t1.reshape(256, 128), t2.reshape(256, 128)], axis=0) / NZ
 
     def parts(x):
@@ -123,7 +123,7 @@
         np.concatenate([xh, xh, xl], axis=2),
         np.concatenate([fh, fl], axis=1),
         np.concatenate([gh, gl], axis=0),
-        parts(back),
+        np.concatenate(list(parts(back)), axis=1),
     )
 
 
@@ -131,7 +131,7 @@
     orb_h, cols_h, deps_h, pot_h, proj_h, atoms_h, coup_h, slab_h, tz_h, turn_h, wiy_h, wix_h, wfy_h, wfx_h, tback_h,
     out, out_sums,
     orb, cols, deps, pot, proj, atoms, coup, slab, tz, turn, wiy, wix, wfy, wfx, tback,
-    mine, got, tiles, ret, pool, red, nonl, vecs, field_pot,
+    mine, got, tiles, ret, pool, red, nonl, vecs, field_pot, angles, work,
     loads, sa, ra, sb, rb, near_s, near_r, far_s, far_r, sf, rf, sr, rr,
 ):
     me = lax.axis_index("fft")
@@ -267,6 +267,9 @@
     ]
     for c in near:
         c.start()
+
+    angles[0] = cosp.T[:STK]
+    angles[1] = sinp.T[:STK]
 
     sr_i = lax.broadcasted_iota(jnp.int32, (16, STK), 1) // 2
     rr_i = lax.broadcasted_iota(jnp.int32, (16, STK), 0)
@@ -399,8 +402,8 @@
     near[3].wait_recv()
     far[5].start()
 
-    fwd_y = mm(hi, wfy[...]) + mm(lo, wfy[...])
-    fwd_y = fwd_y[:, :128] + fwd_y[:, 128:]
+    fwd_y = mm(hi, wfy[...])
+    fwd_y = fwd_y[:, :128] + (fwd_y[:, 128:] + mm(lo, wfy[:, 0:128]))
     stack = []
     for z in range(PLANES):
         right = jnp.concatenate([fwd_y[4 * z * U : (4 * z + 2) * U], fwd_y[(4 * z + 2) * U : (4 * z + 4) * U]], axis=1)
@@ -467,32 +470,36 @@
         pool.at[core], pool.at[core], sf, rf, device_id={"band": twin}, device_id_type=MESH
     )
 
-    def correlate(at):
-        def step(r, carry):
+    def correlate(at, half):
+        def step(r4, carry):
             u, w = carry
-            block = pool[:, :, :, pl.ds(pl.multiple_of(128 * r, 128), 128)]
-            u = u + block * vecs[at, pl.ds(r, 1), :]
-            w = w + block * vecs[at + 1, pl.ds(r, 1), :]
+            for r in range(4):
+                block = pool[half, :, :, pl.ds(pl.multiple_of(512 * r4 + 128 * r, 128), 128)]
+                u = u + block * vecs[at, pl.ds(4 * r4 + r, 1), :]
+                w = w + block * vecs[at + 1, pl.ds(4 * r4 + r, 1), :]
             return u, w
 
-        zero = jnp.zeros((2, 8, 8, 128), F32)
-        u, w = lax.fori_loop(0, 16, step, (zero, zero))
-        real = [u[k % 2, k // 2][0:4] + w[k % 2, k // 2][4:8] for k in range(16)]
-        imag = [w[k % 2, k // 2][0:4] - u[k % 2, k // 2][4:8] for k in range(16)]
-        return mm(ones, jnp.concatenate(real + imag, axis=0), NT, HIGHEST)[0:1, :]
+        zero = jnp.zeros((8, 8, 128), F32)
+        u, w = lax.fori_loop(0, 4, step, (zero, zero))
+        for y in range(8):
+            work[at // 2, half, y, 0:4, :] = u[y, 0:4] + w[y, 4:8]
+            work[at // 2, half, y, 4:8, :] = w[y, 0:4] - u[y, 4:8]
 
     vecs[0] = m_re
     vecs[1] = m_im
     base_re = kin * m_re + nonl[0]
     base_im = kin * m_im + nonl[1]
+    correlate(0, core)
 
     every = pltpu.make_async_remote_copy(
         tiles.at[pl.ds(1, NF - 1)], ret.at[pl.ds(0, NF - 1)], sb, rb, device_id={"fft": fft_at(0, 1)}, device_id_type=MESH
     )
     every.wait_recv()
-    came = jnp.concatenate([ret[d] for d in range(NF)], axis=0)
-    came = jnp.concatenate([came] + [pltpu.roll(came, 128 - 32 * q, 1) for q in range(1, 4)], axis=0)
-    loc = mm_left(tback, jnp.concatenate([came * cosp, came * sinp], axis=0)).T
+    came = jnp.concatenate([ret[d] for d in range(NF)], axis=0).T
+    came = jnp.concatenate([came[STK * q : STK * (q + 1)] for q in range(4)], axis=1)
+    hi, lo = split(jnp.concatenate([came * angles[0], came * angles[1]], axis=1))
+    loc = mm(jnp.concatenate([hi, lo], axis=0), tback[...])
+    loc = loc[:STK, :128] + (loc[:STK, 128:] + loc[STK:, :128])
     loc_re = jnp.concatenate([loc[0:16, :GZ], loc[16:32, :GZ]], axis=1)
     loc_im = jnp.concatenate([loc[0:16, GZ:], loc[16:32, GZ:]], axis=1)
     a_re = jnp.where(mask, base_re + loc_re, 0.0)
@@ -501,10 +508,20 @@
     vecs[3] = a_im
     out[0] = a_re
     out[1] = a_im
+    correlate(2, core)
     swap.wait_recv()
-    s_row = correlate(0)
-    h_row = correlate(2)
-    red[me] = jnp.concatenate([h_row, s_row], axis=0)
+    correlate(0, 1 - core)
+    correlate(2, 1 - core)
+    order = [(c, k) for c in range(2) for k in range(16)]
+    full = jnp.concatenate(
+        [work[t, k % 2, k // 2, 4 * c : 4 * c + 4, :] for t in (1, 0) for c, k in order], axis=0
+    )
+    hi = full.astype(BF16)
+    rest = full - hi.astype(F32)
+    mid, lo = split(rest)
+    one = jnp.ones((8, 128), BF16)
+    sums = mm(one, hi, NT) + (mm(one, mid, NT) + mm(one, lo, NT))
+    red[me] = jnp.concatenate([sums[0:1, :128], sums[0:1, 128:]], axis=0)
     for dz, dx in OFFSETS:
         pltpu.make_async_remote_copy(
             red.at[me], red.at[me], sr, rr, device_id={"fft": fft_at(dz, dx)}, device_id_type=MESH
@@ -562,6 +579,8 @@
             pltpu.VMEM((2, 16, 128), F32),
             pltpu.VMEM((4, 16, 128), F32),
             pltpu.VMEM((2, 8 * U, 128), F32),
+            pltpu.VMEM((2, STK, 256), F32),
+            pltpu.VMEM((2, 2, 8, 8, 128), F32),
             dma((len(args),)),
         ]
         + [dma] * 4

time: 36.9 us -> 36 us (0.976)
  Pallas kernels: 36.1 us -> 35.2 us
    pallas_call x1, Pallas kernels: 35.5 us -> 34.5 us  [shards(): pl.pallas_call(kernel, out_shape=(pltpu.VMEM((2, 16, 128), F32), pltpu.VM...]
where the time goes in v5:
time: 36 us; the launch traced here: 35.8 us
  Pallas kernels  35.2 us (98%)
  between operations  0.64 us (2%)
    pallas_call x1, Pallas kernels, shards(): pl.pallas_call(kernel, out_shape=(pltpu.VMEM((2, 16, 128), F32), pltpu.VM...  34.5 us

profile of v5, /device:TPU:1, one launch (start us, length us, event | category | flops | bytes accessed | tf_op | source)
XLA Modules:
  0.0 35.8 jit_solution(15024412036677792937)
XLA Ops:
  0.6 34.5 %davidson.1 = (f32[2,16,128]{2,1,0:T(8,128)S(1)}, f32[2,128]{1,0:T(2,128)S(1)}) custom-call(f32[2,16,128]{2,1,0:T(8,128)} %bitcast.3, s32[1,32]{1,0:T(1,128)} %bitcast.4, s32[32,64]{1,0:T(8,128)} %deps_h.1, f32[3,32400]{1,0:T(4,128)} %pot_h.1, f32[2,16,2048]{2,1,0:T(8,128)} %proj_h.1, s32[2,8]{1,0:T(2,128)} %atoms_h.1, f32[2,8,8]{2,1,0:T(8,128)} %coup_h.1, ...), custom_call_target="tpu_custom_call" | custom-call | tf_op jit(solution)/shard_map/davidson/pallas_call | solution.py:566
  35.2 0.6 %finish.1 = (f32[2,16,128]{2,1,0:T(8,128)}, f32[2,1,64]{2,1,0:T(1,128)}, f32[2,1,64]{2,1,0:T(1,128)}) custom-call(f32[2,16,128]{2,1,0:T(8,128)S(1)} %get-tuple-element.8.applied, f32[2,128]{1,0:T(2,128)S(1)} %get-tuple-element.9.sums), custom_call_target="tpu_custom_call" | custom-call | tf_op jit(solution)/shard_map/finish/pallas_call | solution.py:594

commit v6 on v5

--- a/solution.py
+++ b/solution.py
@@ -242,7 +242,7 @@
     for dz, dx in OFFSETS:
         to = fft_at(dz, dx)
         pltpu.make_async_remote_copy(
-            mine.at[to], got.at[4 * dz + dx], sa, ra, device_id={"fft": to}, device_id_type=MESH
+            mine.at[to], got.at[4 * dz + dx], sa, ra.at[dz], device_id={"fft": to}, device_id_type=MESH
         ).start()
 
     def to_band(src, dst, send, recv, dy):
@@ -311,45 +311,54 @@
             )
         )
     ]
-    whole = pltpu.make_async_remote_copy(
-        got.at[pl.ds(1, NF - 1)], got.at[pl.ds(1, NF - 1)], sa, ra, device_id={"fft": fft_at(0, 1)}, device_id_type=MESH
-    )
-    whole.wait_recv()
-
-    lane = lax.broadcasted_iota(jnp.int32, (8, 128), 1) // 32
-    parts = [[None] * 4 for _ in range(2)]
-    for h in range(2):
-        for b in range(4):
-            rows = jnp.concatenate([got[4 * a + b, h : h + 1, :] for a in range(8)], axis=0)
-            for q in range(4):
-                shift = 32 * ((b - q) % 4)
-                turned = pltpu.roll(rows, shift, 1) if shift else rows
-                parts[h][q] = turned if b == 0 else jnp.where(lane == b, turned, parts[h][q])
-    fields = [parts[p // 4][p % 4] for p in range(6)]
-    code = parts[1][2]
-    kx_at = jnp.floor(code * (1.0 / 256.0))
-    col_at = code - 256.0 * kx_at
-
+    def arrival(dz):
+        block = got.at[pl.ds(1, 3)] if dz == 0 else got.at[pl.ds(4 * dz, 4)]
+        return pltpu.make_async_remote_copy(
+            block, block, sa, ra.at[dz], device_id={"fft": fft_at(0, 1)}, device_id_type=MESH
+        )
+
+    halves = ((0, 1, 7, 2), (6, 3, 5, 4))
+    lane = lax.broadcasted_iota(jnp.int32, (4, 128), 1) // 32
     ix = lax.broadcasted_iota(jnp.int32, (KA, 128), 0).astype(F32)
     iy = lax.broadcasted_iota(jnp.int32, (4 * KB, 128), 0).astype(F32)
-    his = [f.astype(BF16).astype(F32) for f in fields]
-    los = [f - h for f, h in zip(fields, his)]
-    on = [ix == kx_at[a : a + 1, :] for a in range(8)]
-    hot_y = [(iy == col_at[a : a + 1, :]).astype(F32).astype(BF16) for a in range(8)]
-    wide = [jnp.concatenate(hot_y[a : a + 2], axis=1) for a in range(0, 8, 2)]
-    grid = jnp.zeros((6 * KA, 4 * KB), F32)
-    for a in range(0, 8, 2):
-        for values in (his, los):
-            placed = jnp.concatenate(
-                [
-                    jnp.concatenate(
-                        [jnp.where(on[i], values[p][i : i + 1, :], 0.0).astype(BF16) for i in (a, a + 1)], axis=1
-                    )
-                    for p in range(6)
-                ],
-                axis=0,
-            )
-            grid += mm(placed, wide[a // 2], NT)
+    grid = jnp.zeros((12 * KA, 4 * KB), F32)
+    total = jnp.zeros((1, 128), F32)
+    on, wide = [], []
+    for half_of in halves:
+        for dz in half_of:
+            arrival(dz).wait_recv()
+        parts = [[None] * 4 for _ in range(2)]
+        for h in range(2):
+            for b in range(4):
+                rows = jnp.concatenate([got[4 * a + b, h : h + 1, :] for a in half_of], axis=0)
+                for q in range(4):
+                    shift = 32 * ((b - q) % 4)
+                    turned = pltpu.roll(rows, shift, 1) if shift else rows
+                    parts[h][q] = turned if b == 0 else jnp.where(lane == b, turned, parts[h][q])
+        fields = [parts[p // 4][p % 4] for p in range(6)]
+        total += jnp.sum(parts[1][3], axis=0, keepdims=True)
+        code = parts[1][2]
+        kx_at = jnp.floor(code * (1.0 / 256.0))
+        col_at = code - 256.0 * kx_at
+        his = [f.astype(BF16).astype(F32) for f in fields]
+        los = [f - h for f, h in zip(fields, his)]
+        here = [ix == kx_at[a : a + 1, :] for a in range(4)]
+        hot_y = [(iy == col_at[a : a + 1, :]).astype(F32).astype(BF16) for a in range(4)]
+        placed = jnp.concatenate(
+            [
+                jnp.concatenate(
+                    [jnp.where(here[a], values[p][a : a + 1, :], 0.0).astype(BF16) for a in range(4)], axis=1
+                )
+                for values in (his, los)
+                for p in range(6)
+            ],
+            axis=0,
+        )
+        hot_half = jnp.concatenate(hot_y, axis=1)
+        grid += mm(placed, hot_half, NT)
+        on.append(here)
+        wide.append(hot_half)
+    grid = grid[: 6 * KA] + grid[6 * KA :]
 
     low = lax.broadcasted_iota(jnp.int32, (KA, 2 * KB), 1) < KB
     rows = []
@@ -364,6 +373,22 @@
     hi, lo = split(jnp.concatenate(rows, axis=0))
     inv_y = mm(jnp.concatenate([hi, lo], axis=1), wiy[0:256, :]) + mm(hi, wiy[256:384, :])
 
+    def pass_on(k):
+        block = pool.at[core, lax.rem(row + k, 8)]
+        pltpu.make_async_remote_copy(block, block, sf, rf, device_id={"band": twin}, device_id_type=MESH).start()
+
+    near[0].wait_recv()
+    far[0].start()
+    far[1].start()
+    near[1].wait_recv()
+    far[2].start()
+    far[3].start()
+    near[2].wait_recv()
+    far[4].start()
+    near[3].wait_recv()
+    far[5].start()
+    for k in (0, 2, 6):
+        pass_on(k)
     planes = []
     for z in range(PLANES):
         part4 = [inv_y[(4 * z + i) * KA : (4 * z + i + 1) * KA] for i in range(4)]
@@ -391,16 +416,6 @@
             (e_im - o_re) * value[1],
         ]
     hi, lo = split(jnp.concatenate(planes, axis=0))
-    near[0].wait_recv()
-    far[0].start()
-    far[1].start()
-    near[1].wait_recv()
-    far[2].start()
-    far[3].start()
-    near[2].wait_recv()
-    far[4].start()
-    near[3].wait_recv()
-    far[5].start()
 
     fwd_y = mm(hi, wfy[...])
     fwd_y = fwd_y[:, :128] + (fwd_y[:, 128:] + mm(lo, wfy[:, 0:128]))
@@ -419,31 +434,39 @@
             imag.append(jnp.where(low, n + n_t, n_t - n))
         stack += [jnp.concatenate(real, axis=1), jnp.concatenate(imag, axis=1)]
     hi, lo = split(jnp.concatenate(stack, axis=0))
-    picked = [[] for _ in range(6)]
-    for a in range(0, 8, 2):
-        spread = mm(hi, wide[a // 2]) + mm(lo, wide[a // 2])
-        for i in range(2):
-            for p in range(6):
-                block = spread[p * KA : (p + 1) * KA, 128 * i : 128 * (i + 1)]
-                picked[p].append(jnp.sum(jnp.where(on[a + i], block, 0.0), axis=0, keepdims=True))
-    picked = [jnp.concatenate(rows, axis=0) for rows in picked] + [jnp.zeros((8, 128), F32)] * 2
-    for h in range(2):
-        for b in range(4):
-            rows = None
-            for q in range(4):
-                shift = 32 * ((q - b) % 4)
-                turned = pltpu.roll(picked[4 * h + q], shift, 1) if shift else picked[4 * h + q]
-                rows = turned if q == 0 else jnp.where(lane == q, turned, rows)
-            for a in range(8):
-                tiles[4 * a + b, h : h + 1, :] = rows[a : a + 1, :]
+    both_parts = jnp.concatenate([hi, lo], axis=0)
+    for half_of, here, hot_half in ((halves[1], on[1], wide[1]), (halves[0], on[0], wide[0])):
+        spread = mm(both_parts, hot_half)
+        spread = spread[: 6 * KA] + spread[6 * KA :]
+        picked = []
+        for p in range(6):
+            rows = []
+            for a in range(4):
+                block = spread[p * KA : (p + 1) * KA, 128 * a : 128 * (a + 1)]
+                rows.append(jnp.sum(jnp.where(here[a], block, 0.0), axis=0, keepdims=True))
+            picked.append(jnp.concatenate(rows, axis=0))
+        picked += [jnp.zeros((4, 128), F32)] * 2
+        for h in range(2):
+            for b in range(4):
+                rows = None
+                for q in range(4):
+                    shift = 32 * ((q - b) % 4)
+                    turned = pltpu.roll(picked[4 * h + q], shift, 1) if shift else picked[4 * h + q]
+                    rows = turned if q == 0 else jnp.where(lane == q, turned, rows)
+                for a in range(4):
+                    tiles[4 * half_of[a] + b, h : h + 1, :] = rows[a : a + 1, :]
+        for dz, dx in OFFSETS:
+            if dz in half_of:
+                pltpu.make_async_remote_copy(
+                    tiles.at[4 * dz + dx],
+                    ret.at[me],
+                    sb,
+                    rb,
+                    device_id={"fft": fft_at(8 - dz, 4 - dx)},
+                    device_id_type=MESH,
+                ).start()
     ret[me] = tiles[0]
 
-    for dz, dx in OFFSETS:
-        pltpu.make_async_remote_copy(
-            tiles.at[4 * dz + dx], ret.at[me], sb, rb, device_id={"fft": fft_at(8 - dz, 4 - dx)}, device_id_type=MESH
-        ).start()
-
-    total = jnp.sum(parts[1][3], axis=0, keepdims=True)
     total = total + pltpu.roll(total, 64, 1)
     total = total + pltpu.roll(total, 32, 1)
     c_re = jnp.sum(dfull * total[:, 0:16], axis=1, keepdims=True)
@@ -454,18 +477,19 @@
         nonl[0, r : r + 1, :] = jnp.sum(c_re * p_re - c_im * p_im, axis=0, keepdims=True)
         nonl[1, r : r + 1, :] = jnp.sum(c_re * p_im + c_im * p_re, axis=0, keepdims=True)
 
-    def pass_on(k):
-        block = pool.at[core, lax.rem(row + k, 8)]
-        pltpu.make_async_remote_copy(block, block, sf, rf, device_id={"band": twin}, device_id_type=MESH).start()
-
     near[4].wait_recv()
     near[5].wait_recv()
-    for k in (0, 1, 2, 6, 7):
+    for k in (1, 7):
         pass_on(k)
-    for c in far:
-        c.wait_recv()
-    for k in (3, 4, 5):
-        pass_on(k)
+    far[1].wait_recv()
+    far[4].wait_recv()
+    pass_on(5)
+    far[3].wait_recv()
+    far[5].wait_recv()
+    pass_on(3)
+    far[0].wait_recv()
+    far[2].wait_recv()
+    pass_on(4)
     swap = pltpu.make_async_remote_copy(
         pool.at[core], pool.at[core], sf, rf, device_id={"band": twin}, device_id_type=MESH
     )
@@ -527,7 +551,9 @@
             red.at[me], red.at[me], sr, rr, device_id={"fft": fft_at(dz, dx)}, device_id_type=MESH
         ).start()
 
-    whole.wait_send()
+    pltpu.make_async_remote_copy(
+        got.at[pl.ds(1, NF - 1)], got.at[pl.ds(1, NF - 1)], sa, ra.at[0], device_id={"fft": fft_at(0, 1)}, device_id_type=MESH
+    ).wait_send()
     every.wait_send()
     for c in near:
         c.wait_send()
@@ -583,7 +609,7 @@
             pltpu.VMEM((2, 2, 8, 8, 128), F32),
             dma((len(args),)),
         ]
-        + [dma] * 4
+        + [dma, dma((8,)), dma, dma]
         + [dma((6,))] * 4
         + [dma] * 4,
         compiler_params=pltpu.CompilerParams(

time: 36 us -> 35.7 us (level)
  no operation moved by 1% of the time
where the time goes in v6:
time: 35.7 us; the launch traced here: 35.5 us
  Pallas kernels  34.9 us (98%)
  between operations  0.64 us (2%)
    pallas_call x1, Pallas kernels, shards(): pl.pallas_call(kernel, out_shape=(pltpu.VMEM((2, 16, 128), F32), pltpu.VM...  34.3 us

profile of v6, /device:TPU:1, one launch (start us, length us, event | category | flops | bytes accessed | tf_op | source)
XLA Modules:
  0.0 35.5 jit_solution(9493387007199846854)
XLA Ops:
  0.6 34.3 %davidson.1 = (f32[2,16,128]{2,1,0:T(8,128)S(1)}, f32[2,128]{1,0:T(2,128)S(1)}) custom-call(f32[2,16,128]{2,1,0:T(8,128)} %bitcast.3, s32[1,32]{1,0:T(1,128)} %bitcast.4, s32[32,64]{1,0:T(8,128)} %deps_h.1, f32[3,32400]{1,0:T(4,128)} %pot_h.1, f32[2,16,2048]{2,1,0:T(8,128)} %proj_h.1, s32[2,8]{1,0:T(2,128)} %atoms_h.1, f32[2,8,8]{2,1,0:T(8,128)} %coup_h.1, ...), custom_call_target="tpu_custom_call" | custom-call | tf_op jit(solution)/shard_map/davidson/pallas_call | solution.py:592
  34.9 0.6 %finish.1 = (f32[2,16,128]{2,1,0:T(8,128)}, f32[2,1,64]{2,1,0:T(1,128)}, f32[2,1,64]{2,1,0:T(1,128)}) custom-call(f32[2,16,128]{2,1,0:T(8,128)S(1)} %get-tuple-element.8.applied, f32[2,128]{1,0:T(2,128)S(1)} %get-tuple-element.9.sums), custom_call_target="tpu_custom_call" | custom-call | tf_op jit(solution)/shard_map/finish/pallas_call | solution.py:620

commit v7 on v6

--- a/solution.py
+++ b/solution.py
@@ -509,6 +509,23 @@
             work[at // 2, half, y, 0:4, :] = u[y, 0:4] + w[y, 4:8]
             work[at // 2, half, y, 4:8, :] = w[y, 0:4] - u[y, 4:8]
 
+    def correlate_both(half):
+        def step(r4, carry):
+            carry = list(carry)
+            for r in range(4):
+                block = pool[half, :, :, pl.ds(pl.multiple_of(512 * r4 + 128 * r, 128), 128)]
+                for i in range(4):
+                    carry[i] = carry[i] + block * vecs[i, pl.ds(4 * r4 + r, 1), :]
+            return tuple(carry)
+
+        zero = jnp.zeros((8, 8, 128), F32)
+        made = lax.fori_loop(0, 4, step, (zero,) * 4)
+        for t in range(2):
+            u, w = made[2 * t], made[2 * t + 1]
+            for y in range(8):
+                work[t, half, y, 0:4, :] = u[y, 0:4] + w[y, 4:8]
+                work[t, half, y, 4:8, :] = w[y, 0:4] - u[y, 4:8]
+
     vecs[0] = m_re
     vecs[1] = m_im
     base_re = kin * m_re + nonl[0]
@@ -534,8 +551,7 @@
     out[1] = a_im
     correlate(2, core)
     swap.wait_recv()
-    correlate(0, 1 - core)
-    correlate(2, 1 - core)
+    correlate_both(1 - core)
     order = [(c, k) for c in range(2) for k in range(16)]
     full = jnp.concatenate(
         [work[t, k % 2, k // 2, 4 * c : 4 * c + 4, :] for t in (1, 0) for c, k in order], axis=0

time: 35.7 us -> 35.7 us (level)
  no operation moved by 1% of the time
where the time goes in v7:
time: 35.7 us; the launch traced here: 35.5 us
  Pallas kernels  34.9 us (98%)
  between operations  0.64 us (2%)
    pallas_call x1, Pallas kernels, shards(): pl.pallas_call(kernel, out_shape=(pltpu.VMEM((2, 16, 128), F32), pltpu.VM...  34.2 us

profile of v7, /device:TPU:1, one launch (start us, length us, event | category | flops | bytes accessed | tf_op | source)
XLA Modules:
  0.0 35.5 jit_solution(595811380364623625)
XLA Ops:
  0.6 34.2 %davidson.1 = (f32[2,16,128]{2,1,0:T(8,128)S(1)}, f32[2,128]{1,0:T(2,128)S(1)}) custom-call(f32[2,16,128]{2,1,0:T(8,128)} %bitcast.3, s32[1,32]{1,0:T(1,128)} %bitcast.4, s32[32,64]{1,0:T(8,128)} %deps_h.1, f32[3,32400]{1,0:T(4,128)} %pot_h.1, f32[2,16,2048]{2,1,0:T(8,128)} %proj_h.1, s32[2,8]{1,0:T(2,128)} %atoms_h.1, f32[2,8,8]{2,1,0:T(8,128)} %coup_h.1, ...), custom_call_target="tpu_custom_call" | custom-call | tf_op jit(solution)/shard_map/davidson/pallas_call | solution.py:608
  34.9 0.6 %finish.1 = (f32[2,16,128]{2,1,0:T(8,128)}, f32[2,1,64]{2,1,0:T(1,128)}, f32[2,1,64]{2,1,0:T(1,128)}) custom-call(f32[2,16,128]{2,1,0:T(8,128)S(1)} %get-tuple-element.8.applied, f32[2,128]{1,0:T(2,128)S(1)} %get-tuple-element.9.sums), custom_call_target="tpu_custom_call" | custom-call | tf_op jit(solution)/shard_map/finish/pallas_call | solution.py:636
